TPU v7x, 256 devices: a whole 4x4x8 slice. The times are simulated.
256 devices in a mesh: queue: 16 (over z_lo, x, core), head: 16 (over y, z_hi).
Axes of the slice: x: 4, y: 4, z: 8 (z_hi: 4, z_lo: 2; z = z_hi * 2 + z_lo), core: 2. Of those that a mesh axis runs over, the one named last changes fastest.
Arguments:
- queries: bfloat16 [32768, 4096], P(('queue', 'head'))
- key_proj: bfloat16 [32768, 4096], P(('queue', 'head'))
- value_proj: bfloat16 [32768, 4096], P(('queue', 'head')), may hold values from -6 to 6
- residual: bfloat16 [32768, 4096], P(('queue', 'head')), may hold values from -6 to 6
- query_gain: float32 [4096], replicated, may hold values from 1 to 3
- key_gain: float32 [4096], replicated, may hold values from 1 to 3
- gate_table: float32 [50, 4096], replicated, may hold values from -6 to 6
- noise_level: int32 [64], replicated, may hold values from 0 to 49
- frame_reach: int32 [64], replicated, may hold values from 1 to 4, as said below
Outputs:
- advanced: bfloat16 [32768, 4096], P(('queue', 'head'))
- key_cache: bfloat16 [32768, 4096], P(('queue', 'head'))
- value_cache: bfloat16 [32768, 4096], P(('queue', 'head'))
Inputs may be any that keep to these rules, and one draw needn't show every extreme that they name: `frame_reach`: both 1 and 4 occur among the values.
All inputs are finite; a program needn't handle non-finite values.
Results may differ from a plain program's by a relative error of at most 0.012.
The roundings to bfloat16 on the way count: a program that leaves them out, or rounds other values in their place, can miss the bound.
Values may be sent and summed in bfloat16 or wider, within the bound.
No kernel may reach another device: no remote copies, remote signals or barrier semaphores. Data moves between devices by JAX's collectives and lax.ppermute only.
A program may use at most 128 MiB of HBM per device.

v0:
```python
import math

import jax
import jax.numpy as jnp
from jax import lax
from jax.sharding import PartitionSpec as P

HD = 128
FRAMES_GRP = 4


def shifted(shard, axis, by):
    devices = lax.axis_size(axis)
    pairs = [(i, i + by) for i in range(devices) if 0 <= i + by < devices]
    return lax.ppermute(shard, axis, pairs)


def normalize(token_rows, gain_row):
    values = token_rows.astype(jnp.float32)
    square = jnp.mean(values * values, axis=-1, keepdims=True)
    return (values * lax.rsqrt(square + 1e-06) * gain_row).astype(jnp.bfloat16)


def send_back(result):
    return lax.all_to_all(result, "head", split_axis=0, concat_axis=1, tiled=True)


def attend(
    query_items, key_items, value_items, prior_keys, prior_values, lower_frame, key_frame, key_live
):
    group_rows = query_items.shape[0]
    item_count = query_items.shape[2]
    head_size = query_items.shape[3]
    score_scale = 1.0 / math.sqrt(head_size)
    keys_all = jnp.concatenate([prior_keys[:, 0], key_items[:, 0]], axis=0)
    values_all = jnp.concatenate([prior_values[:, 0], value_items[:, 0]], axis=0)
    block_rows = min(512, group_rows)
    block_count = group_rows // block_rows
    blocks = query_items[:, 0].reshape(block_count, block_rows, item_count, head_size)
    bound_rows = lower_frame.reshape(block_count, block_rows)

    def one_block(block_pair):
        query_block, bound_block = block_pair
        scores = (
            jnp.einsum("qhd,khd->hqk", query_block, keys_all, preferred_element_type=jnp.float32)
            * score_scale
        )
        allowed = (key_frame[None, :] >= bound_block[:, None]) & key_live[None, :]
        scores = jnp.where(allowed[None], scores, -1e30)
        highest = jnp.max(scores, axis=-1, keepdims=True)
        exp_scores = jnp.exp(scores - highest)
        weights = (exp_scores / jnp.sum(exp_scores, axis=-1, keepdims=True)).astype(jnp.bfloat16)
        return jnp.einsum(
            "hqk,khd->qhd", weights, values_all, preferred_element_type=jnp.float32
        ).astype(jnp.bfloat16)

    result = lax.map(one_block, (blocks, bound_rows))
    return result.reshape(group_rows, 1, item_count, head_size)


def shards(
    queries,
    key_proj,
    value_proj,
    residual,
    query_gain,
    key_gain,
    gate_table,
    noise_level,
    frame_reach,
):
    tok_dev, features = queries.shape
    head_count = lax.axis_size("head")
    head_total = features // HD
    per_device = head_total // head_count
    group_rows = tok_dev * head_count
    frame_tok = group_rows // FRAMES_GRP
    queue_pos = lax.axis_index("queue")
    query_norm = normalize(queries, query_gain)
    key_norm = normalize(key_proj, key_gain)
    reach_here = lax.dynamic_slice_in_dim(frame_reach, queue_pos * FRAMES_GRP, FRAMES_GRP, 0)
    query_frame = jnp.arange(group_rows, dtype=jnp.int32) // frame_tok
    frame_slots = jnp.arange(FRAMES_GRP, dtype=jnp.int32)
    reach_rows = jnp.sum(
        jnp.where(query_frame[:, None] == frame_slots[None, :], reach_here[None, :], 0), axis=1
    )
    lower_frame = query_frame - reach_rows
    key_frame = jnp.arange(2 * group_rows, dtype=jnp.int32) // frame_tok - FRAMES_GRP
    key_live = (key_frame >= 0) | (queue_pos > 0)

    def by_heads(token_rows):
        return token_rows.reshape(tok_dev, head_count, per_device, HD)

    query_items = lax.all_to_all(
        by_heads(query_norm), "head", split_axis=1, concat_axis=0, tiled=True
    )
    key_items = lax.all_to_all(by_heads(key_norm), "head", split_axis=1, concat_axis=0, tiled=True)
    value_items = lax.all_to_all(
        by_heads(value_proj), "head", split_axis=1, concat_axis=0, tiled=True
    )
    prior_keys, prior_values = shifted((key_items, value_items), "queue", 1)
    gathered = send_back(
        attend(
            query_items,
            key_items,
            value_items,
            prior_keys,
            prior_values,
            lower_frame,
            key_frame,
            key_live,
        )
    )
    key_cache, value_cache = shifted((key_norm, value_proj), "queue", 1)
    attention = gathered.reshape(tok_dev, features)
    first_row = (queue_pos * head_count + lax.axis_index("head")) * tok_dev
    row_frame = (first_row + jnp.arange(tok_dev, dtype=jnp.int32)) // frame_tok
    frame_total = noise_level.shape[0]
    frame_pick = row_frame[:, None] == jnp.arange(frame_total, dtype=jnp.int32)[None, :]
    row_level = jnp.sum(jnp.where(frame_pick, noise_level[None, :], 0), axis=1)
    level_pick = (
        row_level[:, None] == jnp.arange(gate_table.shape[0], dtype=jnp.int32)[None, :]
    ).astype(jnp.float32)
    gate_rows = jnp.dot(
        level_pick, gate_table, precision=lax.Precision.HIGHEST, preferred_element_type=jnp.float32
    )
    advanced = (residual.astype(jnp.float32) + gate_rows * attention.astype(jnp.float32)).astype(
        jnp.bfloat16
    )
    return (advanced, key_cache, value_cache)


def solution(mesh):
    return jax.shard_map(
        shards,
        mesh=mesh,
        in_specs=(
            P(("queue", "head"), None),
            P(("queue", "head"), None),
            P(("queue", "head"), None),
            P(("queue", "head"), None),
            P(),
            P(),
            P(),
            P(),
            P(),
        ),
        out_specs=(
            P(("queue", "head"), None),
            P(("queue", "head"), None),
            P(("queue", "head"), None),
        ),
        check_vma=False,
    )
```

profile of v0, /device:TPU:7, one launch (start us, length us, event | category | flops | bytes accessed | tf_op | source)
XLA Modules:
  0.0 270.9 jit_solution(2761573572580003086)
XLA Ops:
  3.7 2.1 copy.56
  5.8 10.9 %all-to-all-start.1 = ((bf16[128,16,2,128]{3,2,0,1:T(2,128)(2,1)}), bf16[128,16,2,128]{3,2,0,1:T(2,128)(2,1)S(1)}, u32[]{:S(2)}, u32[]{:S(2)}) async-start(bf16[128,16,2,128]{3,2,0,1:T(2,128)(2,1)} %copy.56), calls=%async_computation.1 | async-start | bytes 2097152 | tf_op jit(solution)/shard_map/all_to_all | solution.py:97
  19.6 23.1 %all-to-all-done.1 = bf16[128,16,2,128]{3,2,0,1:T(2,128)(2,1)S(1)} async-done(((bf16[128,16,2,128]{3,2,0,1:T(2,128)(2,1)}), bf16[128,16,2,128]{3,2,0,1:T(2,128)(2,1)S(1)}, u32[]{:S(2)}, u32[]{:S(2)}) %all-to-all-start.1) | async-done | bytes 1048608 | tf_op jit(solution)/shard_map/all_to_all | solution.py:97
  42.7 6.7 %all-to-all-start.2 = ((bf16[128,16,2,128]{3,0,2,1:T(8,128)(2,1)}), bf16[128,16,2,128]{3,0,2,1:T(8,128)(2,1)}, u32[]{:S(2)}, u32[]{:S(2)}) async-start(bf16[128,16,2,128]{3,0,2,1:T(8,128)(2,1)} %copy.60), calls=%async_computation.2 | async-start | bytes 2097152 | tf_op jit(solution)/shard_map/all_to_all | solution.py:98
  53.2 19.1 %all-to-all-done.2 = bf16[128,16,2,128]{3,0,2,1:T(8,128)(2,1)} async-done(((bf16[128,16,2,128]{3,0,2,1:T(8,128)(2,1)}), bf16[128,16,2,128]{3,0,2,1:T(8,128)(2,1)}, u32[]{:S(2)}, u32[]{:S(2)}) %all-to-all-start.2) | async-done | bytes 1048608 | tf_op jit(solution)/shard_map/all_to_all | solution.py:98
  72.2 4.8 %all-to-all-start = ((bf16[128,16,2,128]{0,3,2,1:T(8,128)(2,1)}), bf16[128,16,2,128]{0,3,2,1:T(8,128)(2,1)S(1)}, u32[]{:S(2)}, u32[]{:S(2)}) async-start(bf16[128,16,2,128]{0,3,2,1:T(8,128)(2,1)} %bitcast.72), calls=%async_computation | async-start | bytes 2097152 | tf_op jit(solution)/shard_map/all_to_all | solution.py:94
  77.0 2.3 copy.61
  79.4 9.9 %collective-permute-start.1 = (bf16[2048,1,2,128]{3,0,2,1:T(8,128)(2,1)}, bf16[2048,1,2,128]{3,0,2,1:T(8,128)(2,1)}, u32[]{:S(2)}, u32[]{:S(2)}) collective-permute-start(bf16[2048,1,2,128]{3,0,2,1:T(8,128)(2,1)} %bitcast.14), channel_id=1, source_target_pairs={{0,16},{16,32},{32,48},{48,64},{64,80},{80,96},{96,112},{112,128},... | collective-permute-start | bytes 3145736 | tf_op jit(solution)/shard_map/ppermute | solution.py:15
  92.7 5.9 %all-to-all-done = bf16[128,16,2,128]{0,3,2,1:T(8,128)(2,1)S(1)} async-done(((bf16[128,16,2,128]{0,3,2,1:T(8,128)(2,1)}), bf16[128,16,2,128]{0,3,2,1:T(8,128)(2,1)S(1)}, u32[]{:S(2)}, u32[]{:S(2)}) %all-to-all-start) | async-done | bytes 1048608 | tf_op jit(solution)/shard_map/all_to_all | solution.py:94
  100.0 11.5 %collective-permute-done.1 = bf16[2048,1,2,128]{3,0,2,1:T(8,128)(2,1)} collective-permute-done((bf16[2048,1,2,128]{3,0,2,1:T(8,128)(2,1)}, bf16[2048,1,2,128]{3,0,2,1:T(8,128)(2,1)}, u32[]{:S(2)}, u32[]{:S(2)}) %collective-permute-start.1) | collective-permute-done | bytes 1048608 | tf_op jit(solution)/shard_map/ppermute | solution.py:15
  111.5 3.0 %pad_maximum_fusion.1 = bf16[4096,2,128]{2,0,1:T(8,128)(2,1)} fusion(bf16[2048,2,128]{2,0,1:T(8,128)(2,1)} %bitcast.17, bf16[2048,2,128]{2,0,1:T(8,128)(2,1)} %bitcast.15), kind=kLoop, calls=%fused_computation.49 | loop fusion | flops 4194304 | bytes 4194304 | tf_op jit(solution)/shard_map/concatenate | solution.py:36
  114.5 8.2 %collective-permute-done = bf16[2048,1,2,128]{3,0,2,1:T(8,128)(2,1)} collective-permute-done((bf16[2048,1,2,128]{3,0,2,1:T(8,128)(2,1)}, bf16[2048,1,2,128]{3,0,2,1:T(8,128)(2,1)}, u32[]{:S(2)}, u32[]{:S(2)}) %collective-permute-start) | collective-permute-done | bytes 1048608 | tf_op jit(solution)/shard_map/ppermute | solution.py:15
  122.8 2.7 pad_maximum_fusion
  125.4 86.0 %while.11 = (s32[]{:T(128)}, bf16[4,512,2,128]{3,1,0,2:T(8,128)(2,1)}, s32[4,512]{1,0:T(4,128)S(1)}, bf16[4,512,2,128]{3,1,0,2:T(8,128)(2,1)}, bf16[4096,2,128]{...) while((s32[]{:T(128)}, bf16[4,512,2,128]{3,1,0,2:T(8,128)(2,1)}, ...), condition=%wide.region_7.8_spmd.clone, body=%wide.region_4.7_spmd.clone.sunk | while | flops 2177060864 | bytes 42522728 | solution.py:57
  127.0 10.5 %fusion.71 = (f32[2,512]{1,0:T(2,128)S(1)}, f32[2,512,4096]{2,1,0:T(8,128)}) fusion(pred[512,4096]{1,0:T(8,128)(4,1)S(1)} %compare_and_fusion.2, bf16[4096,2,128]{2,0,1:T(8,128)(2,1)} %get-tuple-element.188, bf16[4,512,2,128]{3,1,0,2:T(8,128)(2,1)} %get-tuple-element.187, s32[]{:T(128)S(6)} %copy.74), kind=kOutput, calls=%fused_computation.80.clone.1 | convolution fusion | flops 1090523136 | bytes 21237764 | tf_op jit(solution)/shard_map/while/body/eval_jaxpr/sub | solution.py:51
  137.5 9.4 %fusion.72 = bf16[4,512,2,128]{3,1,0,2:T(8,128)(2,1)} fusion(bf16[4,512,2,128]{3,1,0,2:T(8,128)(2,1)} %get-tuple-element.177, s32[]{:T(128)S(6)} %copy.74, bf16[4096,2,128]{2,0,1:T(8,128)(2,1)} %get-tuple-element.189, f32[2,512,4096]{2,1,0:T(8,128)} %get-tuple-element.166, f32[2,512]{1,0:T(2,128)S(1)} %get-tuple-element.167), kind=kOutput, calls=%fused_computation.15.clone.1 | convolution fusion | flops 1082261504 | bytes 19140612 | tf_op jit(solution)/shard_map/while/body/eval_jaxpr/hqk,khd->qhd/dot_general | solution.py:53
  148.4 10.5 %fusion.71 = (f32[2,512]{1,0:T(2,128)S(1)}, f32[2,512,4096]{2,1,0:T(8,128)}) fusion(pred[512,4096]{1,0:T(8,128)(4,1)S(1)} %compare_and_fusion.2, bf16[4096,2,128]{2,0,1:T(8,128)(2,1)} %get-tuple-element.188, bf16[4,512,2,128]{3,1,0,2:T(8,128)(2,1)} %get-tuple-element.187, s32[]{:T(128)S(6)} %copy.74), kind=kOutput, calls=%fused_computation.80.clone.1 | convolution fusion | flops 1090523136 | bytes 21237764 | tf_op jit(solution)/shard_map/while/body/eval_jaxpr/sub | solution.py:51
  159.0 9.4 %fusion.72 = bf16[4,512,2,128]{3,1,0,2:T(8,128)(2,1)} fusion(bf16[4,512,2,128]{3,1,0,2:T(8,128)(2,1)} %get-tuple-element.177, s32[]{:T(128)S(6)} %copy.74, bf16[4096,2,128]{2,0,1:T(8,128)(2,1)} %get-tuple-element.189, f32[2,512,4096]{2,1,0:T(8,128)} %get-tuple-element.166, f32[2,512]{1,0:T(2,128)S(1)} %get-tuple-element.167), kind=kOutput, calls=%fused_computation.15.clone.1 | convolution fusion | flops 1082261504 | bytes 19140612 | tf_op jit(solution)/shard_map/while/body/eval_jaxpr/hqk,khd->qhd/dot_general | solution.py:53
  169.9 10.5 %fusion.71 = (f32[2,512]{1,0:T(2,128)S(1)}, f32[2,512,4096]{2,1,0:T(8,128)}) fusion(pred[512,4096]{1,0:T(8,128)(4,1)S(1)} %compare_and_fusion.2, bf16[4096,2,128]{2,0,1:T(8,128)(2,1)} %get-tuple-element.188, bf16[4,512,2,128]{3,1,0,2:T(8,128)(2,1)} %get-tuple-element.187, s32[]{:T(128)S(6)} %copy.74), kind=kOutput, calls=%fused_computation.80.clone.1 | convolution fusion | flops 1090523136 | bytes 21237764 | tf_op jit(solution)/shard_map/while/body/eval_jaxpr/sub | solution.py:51
  180.5 9.4 %fusion.72 = bf16[4,512,2,128]{3,1,0,2:T(8,128)(2,1)} fusion(bf16[4,512,2,128]{3,1,0,2:T(8,128)(2,1)} %get-tuple-element.177, s32[]{:T(128)S(6)} %copy.74, bf16[4096,2,128]{2,0,1:T(8,128)(2,1)} %get-tuple-element.189, f32[2,512,4096]{2,1,0:T(8,128)} %get-tuple-element.166, f32[2,512]{1,0:T(2,128)S(1)} %get-tuple-element.167), kind=kOutput, calls=%fused_computation.15.clone.1 | convolution fusion | flops 1082261504 | bytes 19140612 | tf_op jit(solution)/shard_map/while/body/eval_jaxpr/hqk,khd->qhd/dot_general | solution.py:53
  191.4 10.5 %fusion.71 = (f32[2,512]{1,0:T(2,128)S(1)}, f32[2,512,4096]{2,1,0:T(8,128)}) fusion(pred[512,4096]{1,0:T(8,128)(4,1)S(1)} %compare_and_fusion.2, bf16[4096,2,128]{2,0,1:T(8,128)(2,1)} %get-tuple-element.188, bf16[4,512,2,128]{3,1,0,2:T(8,128)(2,1)} %get-tuple-element.187, s32[]{:T(128)S(6)} %copy.74), kind=kOutput, calls=%fused_computation.80.clone.1 | convolution fusion | flops 1090523136 | bytes 21237764 | tf_op jit(solution)/shard_map/while/body/eval_jaxpr/sub | solution.py:51
  201.9 9.4 %fusion.72 = bf16[4,512,2,128]{3,1,0,2:T(8,128)(2,1)} fusion(bf16[4,512,2,128]{3,1,0,2:T(8,128)(2,1)} %get-tuple-element.177, s32[]{:T(128)S(6)} %copy.74, bf16[4096,2,128]{2,0,1:T(8,128)(2,1)} %get-tuple-element.189, f32[2,512,4096]{2,1,0:T(8,128)} %get-tuple-element.166, f32[2,512]{1,0:T(2,128)S(1)} %get-tuple-element.167), kind=kOutput, calls=%fused_computation.15.clone.1 | convolution fusion | flops 1082261504 | bytes 19140612 | tf_op jit(solution)/shard_map/while/body/eval_jaxpr/hqk,khd->qhd/dot_general | solution.py:53
  211.4 3.7 %copy.64 = bf16[2048,1,2,128]{3,2,1,0:T(2,128)(2,1)} copy(bf16[2048,1,2,128]{3,0,2,1:T(8,128)(2,1)} %bitcast.76) | data formatting | bytes 2097152 | tf_op jit(solution)/shard_map/reshape | solution.py:58
  215.1 9.1 %all-to-all-start.3 = ((bf16[2048,1,2,128]{3,2,1,0:T(2,128)(2,1)}), bf16[2048,1,2,128]{3,2,1,0:T(2,128)(2,1)S(1)}, u32[]{:S(2)}, u32[]{:S(2)}) async-start(bf16[2048,1,2,128]{3,2,1,0:T(2,128)(2,1)} %copy.64), calls=%async_computation.3 | async-start | bytes 2097152 | tf_op jit(solution)/shard_map/all_to_all | solution.py:25
  224.2 6.8 %collective-permute-start.2 = (bf16[128,4096]{0,1:T(8,128)(2,1)S(1)}, bf16[128,4096]{0,1:T(8,128)(2,1)}, u32[]{:S(2)}, u32[]{:S(2)}) collective-permute-start(bf16[128,4096]{0,1:T(8,128)(2,1)S(1)} %copy-done.2), channel_id=1, source_target_pairs={{0,16},{16,32},{32,48},{48,64},{64,80},{80,96},{96,112},{112,128},... | collective-permute-start | bytes 3145736 | tf_op jit(solution)/shard_map/ppermute | solution.py:15
  231.0 2.1 collective-permute-start.3
  233.3 15.2 %collective-permute-done.2 = bf16[128,4096]{0,1:T(8,128)(2,1)} collective-permute-done((bf16[128,4096]{0,1:T(8,128)(2,1)S(1)}, bf16[128,4096]{0,1:T(8,128)(2,1)}, u32[]{:S(2)}, u32[]{:S(2)}) %collective-permute-start.2) | collective-permute-done | bytes 1048608 | tf_op jit(solution)/shard_map/ppermute | solution.py:15
  248.5 2.3 copy.67
  250.8 9.1 %collective-permute-done.3 = bf16[128,4096]{1,0:T(8,128)(2,1)} collective-permute-done((bf16[128,4096]{1,0:T(8,128)(2,1)}, bf16[128,4096]{1,0:T(8,128)(2,1)}, u32[]{:S(2)}, u32[]{:S(2)}) %collective-permute-start.3) | collective-permute-done | bytes 1048608 | tf_op jit(solution)/shard_map/ppermute | solution.py:15
  261.9 2.7 %reshape.141 = f32[128,4096]{1,0:T(8,128)} reshape(f32[128,16,1,2,128]{4,3,1,0,2:T(2,128)S(1)} %copy.66) | data formatting | bytes 4194304 | tf_op jit(solution)/shard_map/convert_element_type | solution.py:127
  264.6 4.0 %fusion.37 = bf16[128,4096]{1,0:T(8,128)(2,1)} fusion(f32[128,4096]{1,0:T(8,128)} %reshape.141, f32[50,4096]{1,0:T(8,128)S(1)} %copy-done, bf16[128,4096]{1,0:T(8,128)(2,1)} %param.14, s32[128]{0:T(128)S(1)} %select_reduce_fusion.1), kind=kOutput, calls=%fused_computation.37 | convolution fusion | flops 316676352 | bytes 5014016 | tf_op jit(solution)/shard_map/dot_general | solution.py:124
  268.6 2.3 copy.81
  (56 shorter events, 22.6 us)
Async XLA Ops:
  0.6 263.9 %copy-start = (f32[50,4096]{1,0:T(8,128)S(1)}, f32[50,4096]{1,0:T(8,128)}, u32[]{:S(2)}) copy-start(f32[50,4096]{1,0:T(8,128)} %param.17) | copy-start | bytes 2457604
  0.6 2.3 copy-start.3
  3.6 2.1 copy-start.1
  5.8 37.0 %all-to-all-start.1 = ((bf16[128,16,2,128]{3,2,0,1:T(2,128)(2,1)}), bf16[128,16,2,128]{3,2,0,1:T(2,128)(2,1)S(1)}, u32[]{:S(2)}, u32[]{:S(2)}) async-start(bf16[128,16,2,128]{3,2,0,1:T(2,128)(2,1)} %copy.56), calls=%async_computation.1 | async-start | bytes 2097152 | tf_op jit(solution)/shard_map/all_to_all | solution.py:97
  42.7 29.5 %all-to-all-start.2 = ((bf16[128,16,2,128]{3,0,2,1:T(8,128)(2,1)}), bf16[128,16,2,128]{3,0,2,1:T(8,128)(2,1)}, u32[]{:S(2)}, u32[]{:S(2)}) async-start(bf16[128,16,2,128]{3,0,2,1:T(8,128)(2,1)} %copy.60), calls=%async_computation.2 | async-start | bytes 2097152 | tf_op jit(solution)/shard_map/all_to_all | solution.py:98
  49.5 2.2 copy-start.4
  72.2 26.4 %all-to-all-start = ((bf16[128,16,2,128]{0,3,2,1:T(8,128)(2,1)}), bf16[128,16,2,128]{0,3,2,1:T(8,128)(2,1)S(1)}, u32[]{:S(2)}, u32[]{:S(2)}) async-start(bf16[128,16,2,128]{0,3,2,1:T(8,128)(2,1)} %bitcast.72), calls=%async_computation | async-start | bytes 2097152 | tf_op jit(solution)/shard_map/all_to_all | solution.py:94
  77.0 15.5 %copy-start.5 = (s32[64]{0:T(128)S(1)}, s32[64]{0:T(128)}, u32[]{:S(2)}) copy-start(s32[64]{0:T(128)} %param.19) | copy-start | bytes 772
  79.4 32.2 %collective-permute-start.1 = (bf16[2048,1,2,128]{3,0,2,1:T(8,128)(2,1)}, bf16[2048,1,2,128]{3,0,2,1:T(8,128)(2,1)}, u32[]{:S(2)}, u32[]{:S(2)}) collective-permute-start(bf16[2048,1,2,128]{3,0,2,1:T(8,128)(2,1)} %bitcast.14), channel_id=1, source_target_pairs={{0,16},{16,32},{32,48},{48,64},{64,80},{80,96},{96,112},{112,128},... | collective-permute-start | bytes 3145736 | tf_op jit(solution)/shard_map/ppermute | solution.py:15
  90.3 32.4 %collective-permute-start = (bf16[2048,1,2,128]{3,0,2,1:T(8,128)(2,1)}, bf16[2048,1,2,128]{3,0,2,1:T(8,128)(2,1)}, u32[]{:S(2)}, u32[]{:S(2)}) collective-permute-start(bf16[2048,1,2,128]{3,0,2,1:T(8,128)(2,1)} %copy.57), channel_id=1, source_target_pairs={{0,16},{16,32},{32,48},{48,64},{64,80},{80,96},{96,112},{112,128},... | collective-permute-start | bytes 3145736 | tf_op jit(solution)/shard_map/ppermute | solution.py:15
  211.4 12.8 %copy-start.2 = (bf16[128,4096]{0,1:T(8,128)(2,1)S(1)}, bf16[128,4096]{0,1:T(8,128)(2,1)}, u32[]{:S(2)}) copy-start(bf16[128,4096]{0,1:T(8,128)(2,1)} %copy-done.1) | copy-start | bytes 3145732
  211.4 21.8 %copy-start.6 = (s32[64]{0:T(128)S(1)}, s32[64]{0:T(128)}, u32[]{:S(2)}) copy-start(s32[64]{0:T(128)} %param.18) | copy-start | bytes 772
  215.1 44.7 %all-to-all-start.3 = ((bf16[2048,1,2,128]{3,2,1,0:T(2,128)(2,1)}), bf16[2048,1,2,128]{3,2,1,0:T(2,128)(2,1)S(1)}, u32[]{:S(2)}, u32[]{:S(2)}) async-start(bf16[2048,1,2,128]{3,2,1,0:T(2,128)(2,1)} %copy.64), calls=%async_computation.3 | async-start | bytes 2097152 | tf_op jit(solution)/shard_map/all_to_all | solution.py:25
  224.2 24.3 %collective-permute-start.2 = (bf16[128,4096]{0,1:T(8,128)(2,1)S(1)}, bf16[128,4096]{0,1:T(8,128)(2,1)}, u32[]{:S(2)}, u32[]{:S(2)}) collective-permute-start(bf16[128,4096]{0,1:T(8,128)(2,1)S(1)} %copy-done.2), channel_id=1, source_target_pairs={{0,16},{16,32},{32,48},{48,64},{64,80},{80,96},{96,112},{112,128},... | collective-permute-start | bytes 3145736 | tf_op jit(solution)/shard_map/ppermute | solution.py:15
  231.0 28.9 %collective-permute-start.3 = (bf16[128,4096]{1,0:T(8,128)(2,1)}, bf16[128,4096]{1,0:T(8,128)(2,1)}, u32[]{:S(2)}, u32[]{:S(2)}) collective-permute-start(bf16[128,4096]{1,0:T(8,128)(2,1)} %param.13), channel_id=1, source_target_pairs={{0,16},{16,32},{32,48},{48,64},{64,80},{80,96},{96,112},{112,128},... | collective-permute-start | bytes 3145736 | tf_op jit(solution)/shard_map/ppermute | solution.py:15
where the time goes:
time: 275 us; the launch traced here: 271 us
  waiting for transfers between devices  92.1 us (33%)
  matrix products  83.9 us (31%)
  starting transfers between devices  52.4 us (19%)
  local copies, waits for them, and re-layouts  26.1 us (9%)
  other arithmetic  15.5 us (6%)
    ppermute x4, waiting for transfers between devices, shifted(): return lax.ppermute(shard, axis, pairs)  44 us
    sub x4, matrix products, one_block(): exp_scores = jnp.exp(scores - highest)  42.1 us
    dot_general x4, matrix products, one_block(): jnp.einsum('hqk,khd->qhd', weights, values_all, preferred_element_type=jn...  37.8 us
    all_to_all x1, waiting for transfers between devices, shards(): lax.all_to_all(by_heads(key_norm), 'head', split_axis=1, concat_axis=0, t...  23.1 us
    ppermute x4, starting transfers between devices, shifted(): return lax.ppermute(shard, axis, pairs)  20.9 us
    all_to_all x1, waiting for transfers between devices, shards(): lax.all_to_all(by_heads(value_proj), 'head', split_axis=1, concat_axis=0,...  19.1 us
    all_to_all x1, starting transfers between devices, shards(): lax.all_to_all(by_heads(key_norm), 'head', split_axis=1, concat_axis=0, t...  10.9 us
    unnamed x19, local copies, waits for them, and re-layouts  9.52 us
  transfers between devices with their start and end apart: 8, of which 7 were waited for; matrix products, arithmetic and copies ran while one was open for 6% of the time, Pallas kernels for 0%

commit v1 on v0

v1 whole, which is shorter than its diff:
```python
import math

import jax
import jax.numpy as jnp
from jax import lax
from jax.experimental import pallas as pl
from jax.experimental.pallas import tpu as pltpu
from jax.sharding import PartitionSpec as P

HD = 128
FRAMES_GRP = 4
FRAME_SLOTS = 4
PREP_ROWS = 32
LOG2E = 1.4426950408889634
SMEM = pltpu.SMEM
VMEM_LIMIT = 48 * 1024 * 1024


def normalize(token_rows, gain_row):
    values = token_rows.astype(jnp.float32)
    square = jnp.mean(values * values, axis=-1, keepdims=True)
    return (values * lax.rsqrt(square + 1e-06) * gain_row).astype(jnp.bfloat16)


def prep_kernel(q_ref, k_ref, v_ref, qg_ref, kg_ref, first_ref, second_ref, key_ref):
    rows, features = q_ref.shape
    query_norm = normalize(q_ref[...], qg_ref[...])
    key_norm = normalize(k_ref[...], kg_ref[...])
    key_ref[...] = key_norm
    for slot, whole in enumerate((v_ref[...], key_norm, query_norm)):
        for head in range(features // HD):
            target = second_ref if head % 2 else first_ref
            target[head // 2, slot] = whole[:, head * HD : (head + 1) * HD]


def prepare(queries, key_proj, value_proj, query_gain, key_gain):
    tok_dev, features = queries.shape
    slots = features // HD // 2
    row_block = pl.BlockSpec((PREP_ROWS, features), lambda i: (i, 0))
    gain_block = pl.BlockSpec((1, features), lambda i: (0, 0))
    item_block = pl.BlockSpec((slots, 3, PREP_ROWS, HD), lambda i: (0, 0, i, 0))
    items = jax.ShapeDtypeStruct((slots, 3, tok_dev, HD), jnp.bfloat16)
    return pl.pallas_call(
        prep_kernel,
        grid=(tok_dev // PREP_ROWS,),
        in_specs=[row_block, row_block, row_block, gain_block, gain_block],
        out_specs=[item_block, item_block, row_block],
        out_shape=[items, items, jax.ShapeDtypeStruct((tok_dev, features), jnp.bfloat16)],
        compiler_params=pltpu.CompilerParams(vmem_limit_bytes=VMEM_LIMIT),
        cost_estimate=pl.CostEstimate(flops=8_000_000, bytes_accessed=8_000_000, transcendentals=0),
        name="prep",
    )(queries, key_proj, value_proj, query_gain.reshape(1, -1), key_gain.reshape(1, -1))


def attend_kernel(place_ref, reach_ref, own_ref, prior_ref, out_ref):
    frame = pl.program_id(0)
    queue_pos = place_ref[0]
    lowest = jnp.where(queue_pos > 0, -FRAMES_GRP, 0)
    lower = jnp.maximum(frame - reach_ref[queue_pos * FRAMES_GRP + frame], lowest)
    rows = FRAME_SLOTS * own_ref.shape[2]
    query = own_ref[pl.ds(frame * FRAME_SLOTS, FRAME_SLOTS), 2].reshape(rows, HD)
    scale = LOG2E / math.sqrt(HD)

    def tile(key, value, carry):
        highest, total, mixed = carry
        scores = lax.dot_general(
            key, query, (((1,), (1,)), ((), ())), preferred_element_type=jnp.float32
        )
        raised = jnp.maximum(highest, jnp.max(scores, axis=0, keepdims=True))
        fade = jnp.exp2((highest - raised) * scale)
        weights = jnp.exp2((scores - raised) * scale)
        total = total * fade + jnp.sum(weights, axis=0, keepdims=True)
        part = lax.dot_general(
            value,
            weights.astype(jnp.bfloat16),
            (((0,), (0,)), ((), ())),
            preferred_element_type=jnp.float32,
        )
        return raised, total, mixed * fade + part

    def own_tile(step, carry):
        at = pl.ds(step * FRAME_SLOTS, FRAME_SLOTS)
        return tile(own_ref[at, 1].reshape(rows, HD), own_ref[at, 0].reshape(rows, HD), carry)

    def prior_tile(step, carry):
        at = pl.ds((step + FRAMES_GRP) * FRAME_SLOTS, FRAME_SLOTS)
        return tile(prior_ref[at, 1].reshape(rows, HD), prior_ref[at, 0].reshape(rows, HD), carry)

    carry = (
        jnp.full((1, rows), -1e30, jnp.float32),
        jnp.zeros((1, rows), jnp.float32),
        jnp.zeros((HD, rows), jnp.float32),
    )
    carry = lax.fori_loop(jnp.maximum(lower, 0), FRAMES_GRP, own_tile, carry)
    carry = lax.fori_loop(jnp.minimum(lower, 0), 0, prior_tile, carry)
    _, total, mixed = carry
    result = (mixed / total).T.astype(jnp.bfloat16)
    out_ref[...] = result.reshape(out_ref.shape)


def attend(place, frame_reach, own, prior):
    slots, _, tok_dev, _ = own.shape
    return pl.pallas_call(
        attend_kernel,
        grid=(FRAMES_GRP,),
        in_specs=[
            pl.BlockSpec(memory_space=SMEM),
            pl.BlockSpec(memory_space=SMEM),
            pl.BlockSpec(own.shape, lambda i: (0, 0, 0, 0)),
            pl.BlockSpec(prior.shape, lambda i: (0, 0, 0, 0)),
        ],
        out_specs=pl.BlockSpec((FRAME_SLOTS, tok_dev, HD), lambda i: (i, 0, 0)),
        out_shape=jax.ShapeDtypeStruct((slots, tok_dev, HD), jnp.bfloat16),
        compiler_params=pltpu.CompilerParams(vmem_limit_bytes=VMEM_LIMIT),
        cost_estimate=pl.CostEstimate(
            flops=4_000_000_000, bytes_accessed=3_000_000, transcendentals=8_000_000
        ),
        name="attend",
    )(place, frame_reach, own, prior)


def finish_kernel(place_ref, level_ref, first_ref, second_ref, residual_ref, gate_ref, out_ref):
    level = level_ref[place_ref[0] * FRAMES_GRP + place_ref[1] // FRAME_SLOTS]
    gate = gate_ref[pl.ds(level, 1), :]
    for head in range(residual_ref.shape[1] // HD):
        source = second_ref if head % 2 else first_ref
        at = slice(head * HD, (head + 1) * HD)
        mixed = gate[:, at] * source[head // 2].astype(jnp.float32)
        out_ref[:, at] = (residual_ref[:, at].astype(jnp.float32) + mixed).astype(jnp.bfloat16)


def finish(place, noise_level, first, second, residual, gate_table):
    tok_dev, features = residual.shape
    blocks = 4
    wide = features // blocks
    slots = first.shape[0] // blocks
    item_block = pl.BlockSpec((slots, tok_dev, HD), lambda i: (i, 0, 0))
    row_block = pl.BlockSpec((tok_dev, wide), lambda i: (0, i))
    return pl.pallas_call(
        finish_kernel,
        grid=(blocks,),
        in_specs=[
            pl.BlockSpec(memory_space=SMEM),
            pl.BlockSpec(memory_space=SMEM),
            item_block,
            item_block,
            row_block,
            pl.BlockSpec((gate_table.shape[0], wide), lambda i: (0, i)),
        ],
        out_specs=row_block,
        out_shape=jax.ShapeDtypeStruct(residual.shape, jnp.bfloat16),
        compiler_params=pltpu.CompilerParams(vmem_limit_bytes=VMEM_LIMIT),
        name="finish",
    )(place, noise_level, first, second, residual, gate_table)


def shifted(shard):
    devices = lax.axis_size("queue")
    return lax.ppermute(shard, "queue", [(i, i + 1) for i in range(devices - 1)])


def exchange(items):
    return lax.all_to_all(items, "head", split_axis=0, concat_axis=0, tiled=True)


def shards(
    queries,
    key_proj,
    value_proj,
    residual,
    query_gain,
    key_gain,
    gate_table,
    noise_level,
    frame_reach,
):
    place = jnp.stack([lax.axis_index("queue"), lax.axis_index("head")]).astype(jnp.int32)
    first, second, key_norm = prepare(queries, key_proj, value_proj, query_gain, key_gain)
    own_first = exchange(first)
    prior_first = shifted(own_first[:, :2])
    own_second = exchange(second)
    prior_second = shifted(own_second[:, :2])
    value_cache = shifted(value_proj)
    key_cache = shifted(key_norm)
    out_first = exchange(attend(place, frame_reach, own_first, prior_first))
    out_second = exchange(attend(place, frame_reach, own_second, prior_second))
    advanced = finish(place, noise_level, out_first, out_second, residual, gate_table)
    return (advanced, key_cache, value_cache)


def solution(mesh):
    return jax.shard_map(
        shards,
        mesh=mesh,
        in_specs=(
            P(("queue", "head"), None),
            P(("queue", "head"), None),
            P(("queue", "head"), None),
            P(("queue", "head"), None),
            P(),
            P(),
            P(),
            P(),
            P(),
        ),
        out_specs=(
            P(("queue", "head"), None),
            P(("queue", "head"), None),
            P(("queue", "head"), None),
        ),
        check_vma=False,
    )
```

time: 275 us -> 195 us (0.71); the launches traced: 271 us -> 194 us
  matrix products: 83.9 us -> 0 us
  blocking collectives: 0 us -> 49.2 us
  waiting for transfers between devices: 92.1 us -> 43 us
  Pallas kernels: 0 us -> 42.6 us
  other arithmetic: 15.5 us -> 0.08 us
  local copies, waits for them, and re-layouts: 26.1 us -> 12.6 us
  starting transfers between devices: 52.4 us -> 46 us
    all_to_all x0 -> x1, blocking collectives: none -> 49.2 us  [exchange(): lax.all_to_all(items, 'head', split_axis=0, concat_axis=0, tiled=True)]
    ppermute x4, waiting for transfers between devices: 44 us -> 0.33 us  [shifted(): lax.ppermute(shard, 'queue', [(i, i + 1) for i in range(devices - 1)])]
    pallas_call x0 -> x4, Pallas kernels: none -> 42.6 us  [the longest x2 37.4 us: attend(): pl.pallas_call(attend_kernel, grid=(FRAMES_GRP,), in_specs=[pl.BlockSpec(...]
    sub x4 -> x0, matrix products: 42.1 us -> none  [one_block(): exp_scores = jnp.exp(scores - highest)]
    dot_general x5 -> x0, matrix products: 41.8 us -> none  [the longest x4 37.8 us: one_block(): jnp.einsum('hqk,khd->qhd', weights, values_all, preferred_element_type=jn...]
    all_to_all x4 -> x3, starting transfers between devices: 31.5 us -> 23.7 us  [exchange(): lax.all_to_all(items, 'head', split_axis=0, concat_axis=0, tiled=True)]
    reshape x3 -> x0, local copies, waits for them, and re-layouts: 7.12 us -> none  [the longest x1 3.7 us: attend(): return result.reshape(group_rows, 1, item_count, head_size)]
    and x4 -> x0, other arithmetic: 5.98 us -> none  [one_block(): allowed = (key_frame[None, :] >= bound_block[:, None]) & key_live[None, :]]
  transfers between devices with their start and end apart: 8 -> 7, of which waited for: 7 -> 3; matrix products, arithmetic and copies ran while one was open for 6% -> 1% of each run, Pallas kernels for 0% -> 19%
where the time goes in v1:
time: 195 us; the launch traced here: 194 us
  blocking collectives  49.2 us (25%)
  starting transfers between devices  46 us (24%)
  waiting for transfers between devices  43 us (22%)
  Pallas kernels  42.6 us (22%)
  local copies, waits for them, and re-layouts  12.6 us (6%)
    all_to_all x1, blocking collectives, exchange(): lax.all_to_all(items, 'head', split_axis=0, concat_axis=0, tiled=True)  49.2 us
    all_to_all x3, waiting for transfers between devices, exchange(): lax.all_to_all(items, 'head', split_axis=0, concat_axis=0, tiled=True)  42.6 us
    pallas_call x2, Pallas kernels, attend(): pl.pallas_call(attend_kernel, grid=(FRAMES_GRP,), in_specs=[pl.BlockSpec(...  37.4 us
    all_to_all x3, starting transfers between devices, exchange(): lax.all_to_all(items, 'head', split_axis=0, concat_axis=0, tiled=True)  23.7 us
    ppermute x4, starting transfers between devices, shifted(): lax.ppermute(shard, 'queue', [(i, i + 1) for i in range(devices - 1)])  22.3 us
    unnamed x26, local copies, waits for them, and re-layouts  10.5 us
  transfers between devices with their start and end apart: 7, of which 3 were waited for; matrix products, arithmetic and copies ran while one was open for 1% of the time, Pallas kernels for 19%

profile of v1, /device:TPU:7, one launch (start us, length us, event | category | flops | bytes accessed | tf_op | source)
XLA Modules:
  0.0 194.2 jit_solution(3112433571356763705)
XLA Ops:
  0.6 1.2 copy-done.1
  1.9 1.2 copy-done.2
  3.1 1.2 copy-done.3
  4.3 0.7 copy-done.7
  5.0 0.7 copy-done.8
  5.7 2.7 %prep.1 = (bf16[16,3,128,128]{3,2,1,0:T(8,128)(2,1)S(1)}, bf16[16,3,128,128]{3,2,1,0:T(8,128)(2,1)}, bf16[128,4096]{1,0:T(8,128)(2,1)S(1)}) custom-call(bf16[128,4096]{1,0:T(8,128)(2,1)S(1)} %copy-done.1, bf16[128,4096]{1,0:T(8,128)(2,1)S(1)} %copy-done.2, bf16[128,4096]{1,0:T(8,128)(2,1)S(1)} %copy-done.3, f32[1,4096]{1,0:T(1,128)S(1)} %bitcast.4, ...), custom_call_target="tpu_custom_call" | custom-call | flops 8000000 | bytes 8000000 | tf_op jit(solution)/shard_map/prep/pallas_call | solution.py:43
  8.5 49.2 %all_to_all.20.own_ref = bf16[16,3,128,128]{3,2,1,0:T(8,128)(2,1)S(1)} all-to-all(bf16[16,3,128,128]{3,2,1,0:T(8,128)(2,1)} %get-tuple-element.7), channel_id=1, replica_groups=mesh['queue'=16,'head'=16] {'head'}, dimensions={0} | all-to-all | bytes 3145728 | tf_op jit(solution)/shard_map/all_to_all | solution.py:163
  57.7 5.5 %all-to-all-start = ((bf16[16,3,128,128]{3,2,1,0:T(8,128)(2,1)}), bf16[16,3,128,128]{3,2,1,0:T(8,128)(2,1)S(1)}, u32[]{:S(2)}, u32[]{:S(2)}) async-start(bf16[16,3,128,128]{3,2,1,0:T(8,128)(2,1)} %copy-done), calls=%async_computation | async-start | bytes 3145728 | tf_op jit(solution)/shard_map/all_to_all | solution.py:163
  63.2 1.0 slice.9
  64.2 4.3 %collective-permute-start.1 = (bf16[16,2,128,128]{3,2,1,0:T(8,128)(2,1)}, bf16[16,2,128,128]{3,2,1,0:T(8,128)(2,1)}, u32[]{:S(2)}, u32[]{:S(2)}) collective-permute-start(bf16[16,2,128,128]{3,2,1,0:T(8,128)(2,1)} %slice.9), channel_id=1, source_target_pairs={{0,16},{16,32},{32,48},{48,64},{64,80},{80,96},{96,112},{112,128},... | collective-permute-start | bytes 3145736 | tf_op jit(solution)/shard_map/ppermute | solution.py:159
  68.5 26.8 %all-to-all-done.own_ref = bf16[16,3,128,128]{3,2,1,0:T(8,128)(2,1)S(1)} async-done(((bf16[16,3,128,128]{3,2,1,0:T(8,128)(2,1)}), bf16[16,3,128,128]{3,2,1,0:T(8,128)(2,1)S(1)}, u32[]{:S(2)}, u32[]{:S(2)}) %all-to-all-start) | async-done | bytes 1572896 | tf_op jit(solution)/shard_map/all_to_all | solution.py:163
  95.3 1.0 slice.8
  96.4 12.2 %collective-permute-start = (bf16[16,2,128,128]{3,2,1,0:T(8,128)(2,1)}, bf16[16,2,128,128]{3,2,1,0:T(8,128)(2,1)}, u32[]{:S(2)}, u32[]{:S(2)}) collective-permute-start(bf16[16,2,128,128]{3,2,1,0:T(8,128)(2,1)} %slice.8), channel_id=1, source_target_pairs={{0,16},{16,32},{32,48},{48,64},{64,80},{80,96},{96,112},{112,128},... | collective-permute-start | bytes 3145736 | tf_op jit(solution)/shard_map/ppermute | solution.py:159
  108.5 0.1 pad_add_fusion.place_ref
  108.6 0.3 collective-permute-done.1.prior_ref
  108.9 18.3 %attend.3 = bf16[16,128,128]{2,1,0:T(8,128)(2,1)S(1)} custom-call(s32[2]{0:T(128)S(1)} %pad_add_fusion.place_ref, s32[64]{0:T(128)S(1)} %copy-done.11, bf16[16,3,128,128]{3,2,1,0:T(8,128)(2,1)S(1)} %all_to_all.20.own_ref, bf16[16,2,128,128]{3,2,1,0:T(8,128)(2,1)} %collective-permute-done.1.prior_ref), custom_call_target="tpu_custom_call" | custom-call | flops 4000000000 | bytes 3000000 | tf_op jit(solution)/shard_map/attend/pallas_call | solution.py:103
  127.3 0.0 copy-start.6
  127.3 0.8 copy-done.6
  128.1 8.8 %all-to-all-start.3 = ((bf16[16,128,128]{2,1,0:T(8,128)(2,1)}), bf16[16,128,128]{2,1,0:T(8,128)(2,1)S(1)}, u32[]{:S(2)}, u32[]{:S(2)}) async-start(bf16[16,128,128]{2,1,0:T(8,128)(2,1)} %copy-done.6), calls=%async_computation.3 | async-start | bytes 1048576 | tf_op jit(solution)/shard_map/all_to_all | solution.py:163
  136.9 3.9 %collective-permute-start.3 = (bf16[128,4096]{1,0:T(8,128)(2,1)}, bf16[128,4096]{1,0:T(8,128)(2,1)}, u32[]{:S(2)}, u32[]{:S(2)}) collective-permute-start(bf16[128,4096]{1,0:T(8,128)(2,1)} %v_ref.1), channel_id=1, source_target_pairs={{0,16},{16,32},{32,48},{48,64},{64,80},{80,96},{96,112},{112,128},... | collective-permute-start | bytes 3145736 | tf_op jit(solution)/shard_map/ppermute | solution.py:159
  140.8 0.0 copy-start.9
  140.8 1.9 collective-permute-start.2
  142.7 0.0 collective-permute-done.prior_ref
  142.7 0.0 copy-start.5
  142.7 19.1 %attend.2 = bf16[16,128,128]{2,1,0:T(8,128)(2,1)} custom-call(s32[2]{0:T(128)S(1)} %pad_add_fusion.place_ref, s32[64]{0:T(128)S(1)} %copy-done.11, bf16[16,3,128,128]{3,2,1,0:T(8,128)(2,1)S(1)} %all-to-all-done.own_ref, bf16[16,2,128,128]{3,2,1,0:T(8,128)(2,1)} %collective-permute-done.prior_ref), custom_call_target="tpu_custom_call" | custom-call | flops 4000000000 | bytes 3000000 | tf_op jit(solution)/shard_map/attend/pallas_call | solution.py:103
  161.8 0.0 all-to-all-done.3.second_ref
  161.8 9.5 %all-to-all-start.1 = ((bf16[16,128,128]{2,1,0:T(8,128)(2,1)}), bf16[16,128,128]{2,1,0:T(8,128)(2,1)S(1)}, u32[]{:S(2)}, u32[]{:S(2)}) async-start(bf16[16,128,128]{2,1,0:T(8,128)(2,1)} %attend.2), calls=%async_computation.1 | async-start | bytes 1048576 | tf_op jit(solution)/shard_map/all_to_all | solution.py:163
  171.3 0.0 collective-permute-done.2
  171.3 15.8 %all-to-all-done.1.first_ref = bf16[16,128,128]{2,1,0:T(8,128)(2,1)S(1)} async-done(((bf16[16,128,128]{2,1,0:T(8,128)(2,1)}), bf16[16,128,128]{2,1,0:T(8,128)(2,1)S(1)}, u32[]{:S(2)}, u32[]{:S(2)}) %all-to-all-start.1) | async-done | bytes 524320 | tf_op jit(solution)/shard_map/all_to_all | solution.py:163
  187.2 2.4 %finish.1 = bf16[128,4096]{1,0:T(8,128)(2,1)} custom-call(s32[2]{0:T(128)S(1)} %pad_add_fusion.place_ref, s32[64]{0:T(128)S(1)} %copy-done.9, bf16[16,128,128]{2,1,0:T(8,128)(2,1)S(1)} %all-to-all-done.1.first_ref, bf16[16,128,128]{2,1,0:T(8,128)(2,1)S(1)} %all-to-all-done.3.second_ref, bf16[128,4096]{1,0:T(8,128)(2,1)S(1)} %copy-done.4, ...), custom_call_target="tpu_custom_call" | custom-call | tf_op jit(solution)/shard_map/finish/pallas_call | solution.py:139
  189.6 2.3 %copy.14 = bf16[128,4096]{1,0:T(8,128)(2,1)} copy(bf16[128,4096]{1,0:T(8,128)(2,1)} %collective-permute-done.2) | data formatting | bytes 2097152
  191.9 2.3 %copy.15 = bf16[128,4096]{1,0:T(8,128)(2,1)} copy(bf16[128,4096]{1,0:T(8,128)(2,1)} %collective-permute-done.3) | data formatting | bytes 2097152
  (16 shorter events, 0.0 us)
Async XLA Ops:
  0.6 1.2 copy-start.1
  1.9 1.2 copy-start.2
  3.1 1.2 copy-start.3
  4.3 0.7 copy-start.7
  5.0 0.7 copy-start.8
  8.5 49.3 %copy-start = (bf16[16,3,128,128]{3,2,1,0:T(8,128)(2,1)}, bf16[16,3,128,128]{3,2,1,0:T(8,128)(2,1)S(1)}, u32[]{:S(2)}) copy-start(bf16[16,3,128,128]{3,2,1,0:T(8,128)(2,1)S(1)} %get-tuple-element.6) | copy-start | bytes 4718596
  8.5 49.3 %copy-start.10 = (bf16[128,4096]{1,0:T(8,128)(2,1)}, bf16[128,4096]{1,0:T(8,128)(2,1)S(1)}, u32[]{:S(2)}) copy-start(bf16[128,4096]{1,0:T(8,128)(2,1)S(1)} %get-tuple-element.8) | copy-start | bytes 3145732
  57.7 37.6 %all-to-all-start = ((bf16[16,3,128,128]{3,2,1,0:T(8,128)(2,1)}), bf16[16,3,128,128]{3,2,1,0:T(8,128)(2,1)S(1)}, u32[]{:S(2)}, u32[]{:S(2)}) async-start(bf16[16,3,128,128]{3,2,1,0:T(8,128)(2,1)} %copy-done), calls=%async_computation | async-start | bytes 3145728 | tf_op jit(solution)/shard_map/all_to_all | solution.py:163
  64.2 44.7 %copy-start.11 = (s32[64]{0:T(128)S(1)}, s32[64]{0:T(128)}, u32[]{:S(2)}) copy-start(s32[64]{0:T(128)} %reach_ref.3) | copy-start | bytes 772
  64.2 44.7 %collective-permute-start.1 = (bf16[16,2,128,128]{3,2,1,0:T(8,128)(2,1)}, bf16[16,2,128,128]{3,2,1,0:T(8,128)(2,1)}, u32[]{:S(2)}, u32[]{:S(2)}) collective-permute-start(bf16[16,2,128,128]{3,2,1,0:T(8,128)(2,1)} %slice.9), channel_id=1, source_target_pairs={{0,16},{16,32},{32,48},{48,64},{64,80},{80,96},{96,112},{112,128},... | collective-permute-start | bytes 3145736 | tf_op jit(solution)/shard_map/ppermute | solution.py:159
  96.4 46.4 %collective-permute-start = (bf16[16,2,128,128]{3,2,1,0:T(8,128)(2,1)}, bf16[16,2,128,128]{3,2,1,0:T(8,128)(2,1)}, u32[]{:S(2)}, u32[]{:S(2)}) collective-permute-start(bf16[16,2,128,128]{3,2,1,0:T(8,128)(2,1)} %slice.8), channel_id=1, source_target_pairs={{0,16},{16,32},{32,48},{48,64},{64,80},{80,96},{96,112},{112,128},... | collective-permute-start | bytes 3145736 | tf_op jit(solution)/shard_map/ppermute | solution.py:159
  127.3 0.8 copy-start.6
  128.1 33.8 %all-to-all-start.3 = ((bf16[16,128,128]{2,1,0:T(8,128)(2,1)}), bf16[16,128,128]{2,1,0:T(8,128)(2,1)S(1)}, u32[]{:S(2)}, u32[]{:S(2)}) async-start(bf16[16,128,128]{2,1,0:T(8,128)(2,1)} %copy-done.6), calls=%async_computation.3 | async-start | bytes 1048576 | tf_op jit(solution)/shard_map/all_to_all | solution.py:163
  136.9 34.5 %collective-permute-start.3 = (bf16[128,4096]{1,0:T(8,128)(2,1)}, bf16[128,4096]{1,0:T(8,128)(2,1)}, u32[]{:S(2)}, u32[]{:S(2)}) collective-permute-start(bf16[128,4096]{1,0:T(8,128)(2,1)} %v_ref.1), channel_id=1, source_target_pairs={{0,16},{16,32},{32,48},{48,64},{64,80},{80,96},{96,112},{112,128},... | collective-permute-start | bytes 3145736 | tf_op jit(solution)/shard_map/ppermute | solution.py:159
  140.8 46.4 %copy-start.9 = (s32[64]{0:T(128)S(1)}, s32[64]{0:T(128)}, u32[]{:S(2)}) copy-start(s32[64]{0:T(128)} %level_ref.1) | copy-start | bytes 772
  140.8 30.5 %collective-permute-start.2 = (bf16[128,4096]{1,0:T(8,128)(2,1)}, bf16[128,4096]{1,0:T(8,128)(2,1)}, u32[]{:S(2)}, u32[]{:S(2)}) collective-permute-start(bf16[128,4096]{1,0:T(8,128)(2,1)} %copy-done.10), channel_id=1, source_target_pairs={{0,16},{16,32},{32,48},{48,64},{64,80},{80,96},{96,112},{112,128},... | collective-permute-start | bytes 3145736 | tf_op jit(solution)/shard_map/ppermute | solution.py:159
  142.7 44.4 %copy-start.5 = (f32[50,4096]{1,0:T(8,128)S(1)}, f32[50,4096]{1,0:T(8,128)}, u32[]{:S(2)}) copy-start(f32[50,4096]{1,0:T(8,128)} %gate_ref.1) | copy-start | bytes 2457604
  161.8 25.3 %copy-start.4 = (bf16[128,4096]{1,0:T(8,128)(2,1)S(1)}, bf16[128,4096]{1,0:T(8,128)(2,1)}, u32[]{:S(2)}) copy-start(bf16[128,4096]{1,0:T(8,128)(2,1)} %residual_ref.1) | copy-start | bytes 3145732
  161.8 25.3 %all-to-all-start.1 = ((bf16[16,128,128]{2,1,0:T(8,128)(2,1)}), bf16[16,128,128]{2,1,0:T(8,128)(2,1)S(1)}, u32[]{:S(2)}, u32[]{:S(2)}) async-start(bf16[16,128,128]{2,1,0:T(8,128)(2,1)} %attend.2), calls=%async_computation.1 | async-start | bytes 1048576 | tf_op jit(solution)/shard_map/all_to_all | solution.py:163

commit v2 on v1

v2 whole, which is shorter than its diff:
```python
import math

import jax
import jax.numpy as jnp
from jax import lax
from jax.experimental import pallas as pl
from jax.experimental.pallas import tpu as pltpu
from jax.sharding import PartitionSpec as P

HD = 128
FRAMES_GRP = 4
FRAME_SLOTS = 4
PREP_ROWS = 32
QUERY_ROWS = 256
WRAP_TO = 8
RELAYS = (None, 0, 3, 5)
LOG2E = 1.4426950408889634
SMEM = pltpu.SMEM
VMEM_LIMIT = 60 * 1024 * 1024


def normalize(token_rows, gain_row):
    values = token_rows.astype(jnp.float32)
    square = jnp.mean(values * values, axis=-1, keepdims=True)
    return (values * lax.rsqrt(square + 1e-06) * gain_row).astype(jnp.bfloat16)


def prep_keys_kernel(k_ref, v_ref, gain_ref, items_ref, key_ref):
    value = v_ref[...]
    key_norm = normalize(k_ref[...], gain_ref[...])
    key_ref[...] = key_norm
    for head in range(k_ref.shape[1] // HD):
        at = slice(head * HD, (head + 1) * HD)
        items_ref[head // 2, 2 * (head % 2)] = value[:, at]
        items_ref[head // 2, 2 * (head % 2) + 1] = key_norm[:, at]


def prep_keys(key_proj, value_proj, key_gain):
    tok_dev, features = key_proj.shape
    slots = features // HD // 2
    row_block = pl.BlockSpec((PREP_ROWS, features), lambda i: (i, 0))
    return pl.pallas_call(
        prep_keys_kernel,
        grid=(tok_dev // PREP_ROWS,),
        in_specs=[row_block, row_block, pl.BlockSpec((1, features), lambda i: (0, 0))],
        out_specs=[pl.BlockSpec((slots, 4, PREP_ROWS, HD), lambda i: (0, 0, i, 0)), row_block],
        out_shape=[
            jax.ShapeDtypeStruct((slots, 4, tok_dev, HD), jnp.bfloat16),
            jax.ShapeDtypeStruct((tok_dev, features), jnp.bfloat16),
        ],
        compiler_params=pltpu.CompilerParams(vmem_limit_bytes=VMEM_LIMIT),
        cost_estimate=pl.CostEstimate(flops=4_000_000, bytes_accessed=5_000_000, transcendentals=0),
        name="prep_keys",
    )(key_proj, value_proj, key_gain.reshape(1, -1))


def prep_queries_kernel(q_ref, gain_ref, items_ref):
    query_norm = normalize(q_ref[...], gain_ref[...])
    for head in range(q_ref.shape[1] // HD):
        items_ref[head // 2, head % 2] = query_norm[:, head * HD : (head + 1) * HD]


def prep_queries(queries, query_gain):
    tok_dev, features = queries.shape
    slots = features // HD // 2
    return pl.pallas_call(
        prep_queries_kernel,
        grid=(tok_dev // PREP_ROWS,),
        in_specs=[
            pl.BlockSpec((PREP_ROWS, features), lambda i: (i, 0)),
            pl.BlockSpec((1, features), lambda i: (0, 0)),
        ],
        out_specs=pl.BlockSpec((slots, 2, PREP_ROWS, HD), lambda i: (0, 0, i, 0)),
        out_shape=jax.ShapeDtypeStruct((slots, 2, tok_dev, HD), jnp.bfloat16),
        compiler_params=pltpu.CompilerParams(vmem_limit_bytes=VMEM_LIMIT),
        cost_estimate=pl.CostEstimate(flops=4_000_000, bytes_accessed=3_000_000, transcendentals=0),
        name="prep_queries",
    )(queries, query_gain.reshape(1, -1))


def attend_kernel(
    place_ref,
    reach_ref,
    query_ref,
    own_value,
    own_key,
    main_ref,
    *refs,
):
    *far_refs, out_ref, mixed_ref, lanes_ref, held_ref, sems = refs
    head, frame = pl.program_id(0), pl.program_id(1)
    queue_pos = place_ref[0]
    lowest = jnp.where(queue_pos > 0, -FRAMES_GRP, 0)
    lower = jnp.maximum(frame - reach_ref[queue_pos * FRAMES_GRP + frame], lowest)
    own_from = jnp.maximum(lower, 0)
    prior_from = jnp.minimum(lower, 0) + FRAMES_GRP
    far = queue_pos == WRAP_TO
    share = held_ref.shape[0] // len(far_refs)

    def loads(source_of):
        for part in range(len(far_refs)):
            at = pl.ds(part * share, share)
            yield pltpu.make_async_copy(source_of(part, at), held_ref.at[at], sems.at[part])

    @pl.when((head == 0) & (frame == 0) & far)
    def _():
        for load in loads(lambda part, at: far_refs[part]):
            load.start()

    @pl.when((head == 0) & (frame == 0) & jnp.logical_not(far))
    def _():
        for load in loads(lambda part, at: main_ref.at[at]):
            load.start()

    prior_value = held_ref.at[:, 2 * head]
    prior_key = held_ref.at[:, 2 * head + 1]
    rows = query_ref.shape[0] * query_ref.shape[1]
    scale = LOG2E / math.sqrt(HD)

    def scores_of(query, key):
        return lax.dot_general(
            query, key, (((1,), (1,)), ((), ())), preferred_element_type=jnp.float32
        )

    def block(ref, start, count):
        slots = ref[pl.ds(start * FRAME_SLOTS, count * FRAME_SLOTS)]
        return slots.reshape(count * rows, HD)

    def plain(key_ref, value_ref, start, add):
        key = block(key_ref, start, FRAMES_GRP - start)
        value = block(value_ref, start, FRAMES_GRP - start)
        query = query_ref[...].reshape(rows, HD)
        for low in range(0, rows, QUERY_ROWS):
            at = slice(low, low + QUERY_ROWS)
            weights = jnp.exp2(scores_of(query[at], key) * scale)
            lanes = lanes_ref[at] if add else 0.0
            for col in range(0, weights.shape[1], HD):
                lanes = lanes + weights[:, col : col + HD]
            mixed = jnp.dot(
                weights.astype(jnp.bfloat16), value, preferred_element_type=jnp.float32
            )
            lanes_ref[at] = lanes
            mixed_ref[at] = mixed_ref[at] + mixed if add else mixed

    for start in range(FRAMES_GRP):

        @pl.when(own_from == start)
        def _(start=start):
            plain(own_key, own_value, start, False)

    @pl.when((head == 0) & (frame == 0))
    def _():
        for load in loads(lambda part, at: main_ref.at[at]):
            load.wait()

    for start in range(FRAMES_GRP):

        @pl.when(prior_from == start)
        def _(start=start):
            plain(prior_key, prior_value, start, True)

    def store(mixed, total):
        out_ref[...] = (mixed / total).astype(jnp.bfloat16).reshape(out_ref.shape)

    total = jnp.sum(lanes_ref[...], axis=1, keepdims=True)
    store(mixed_ref[...], total)
    inside = (jnp.max(total) < 1e37) & (jnp.min(total) > 1e-25)

    @pl.when(jnp.logical_not(inside))
    def _():
        query = query_ref[...].reshape(rows, HD)

        def tile(key, value, carry):
            highest, total, mixed = carry
            scores = scores_of(query, key)
            raised = jnp.maximum(highest, jnp.max(scores, axis=1, keepdims=True))
            fade = jnp.exp2((highest - raised) * scale)
            weights = jnp.exp2((scores - raised) * scale)
            total = total * fade + jnp.sum(weights, axis=1, keepdims=True)
            part = jnp.dot(weights.astype(jnp.bfloat16), value, preferred_element_type=jnp.float32)
            return raised, total, mixed * fade + part

        def own_tile(step, carry):
            return tile(block(own_key, step, 1), block(own_value, step, 1), carry)

        def prior_tile(step, carry):
            return tile(block(prior_key, step, 1), block(prior_value, step, 1), carry)

        start = jnp.full((rows, 1), -1e30, jnp.float32)
        carry = (start, jnp.zeros_like(start), jnp.zeros((rows, HD), jnp.float32))
        carry = lax.fori_loop(own_from, FRAMES_GRP, own_tile, carry)
        _, total, mixed = lax.fori_loop(prior_from, FRAMES_GRP, prior_tile, carry)
        store(mixed, total)


def attend(place, frame_reach, query, own, main, far):
    slots, heads, tok_dev, _ = query.shape
    rows = FRAME_SLOTS * tok_dev
    frame_block = pl.BlockSpec((FRAME_SLOTS, None, tok_dev, HD), lambda h, i: (i, h, 0, 0))
    value_block = pl.BlockSpec((slots, None, tok_dev, HD), lambda h, i: (0, 2 * h, 0, 0))
    key_block = pl.BlockSpec((slots, None, tok_dev, HD), lambda h, i: (0, 2 * h + 1, 0, 0))
    return pl.pallas_call(
        attend_kernel,
        grid=(heads, FRAMES_GRP),
        in_specs=[
            pl.BlockSpec(memory_space=SMEM),
            pl.BlockSpec(memory_space=SMEM),
            frame_block,
            value_block,
            key_block,
            *[pl.BlockSpec(memory_space=pl.ANY) for _ in (main, *far)],
        ],
        out_specs=frame_block,
        out_shape=jax.ShapeDtypeStruct(query.shape, jnp.bfloat16),
        scratch_shapes=[
            pltpu.VMEM((rows, HD), jnp.float32),
            pltpu.VMEM((rows, HD), jnp.float32),
            pltpu.VMEM(main.shape, jnp.bfloat16),
            pltpu.SemaphoreType.DMA((len(far),)),
        ],
        compiler_params=pltpu.CompilerParams(vmem_limit_bytes=VMEM_LIMIT),
        cost_estimate=pl.CostEstimate(
            flops=16_000_000_000, bytes_accessed=6_000_000, transcendentals=16_000_000
        ),
        name="attend",
    )(place, frame_reach, query, own, own, main, *far)


def finish_kernel(
    place_ref,
    gate_ref,
    mixed_ref,
    residual_ref,
    key_main,
    key_late,
    value_main,
    value_late,
    out_ref,
    key_out,
    value_out,
    key_held,
    value_held,
    sems,
):
    step = pl.program_id(0)
    late = (place_ref[0] == WRAP_TO) | (place_ref[0] == 0)
    keys_in = pltpu.make_async_copy(key_main, key_held, sems.at[0])
    late_keys_in = pltpu.make_async_copy(key_late, key_held, sems.at[0])
    values_in = pltpu.make_async_copy(value_main, value_held, sems.at[1])
    late_values_in = pltpu.make_async_copy(value_late, value_held, sems.at[1])
    keys_out = pltpu.make_async_copy(key_held, key_out, sems.at[2])
    values_out = pltpu.make_async_copy(value_held, value_out, sems.at[3])

    @pl.when(step == 0)
    def _():
        @pl.when(late)
        def _():
            late_keys_in.start()
            late_values_in.start()

        @pl.when(jnp.logical_not(late))
        def _():
            keys_in.start()
            values_in.start()

    for head in range(residual_ref.shape[1] // HD):
        at = slice(head * HD, (head + 1) * HD)
        mixed = gate_ref[:, at] * mixed_ref[head // 2, head % 2].astype(jnp.float32)
        out_ref[:, at] = (residual_ref[:, at].astype(jnp.float32) + mixed).astype(jnp.bfloat16)

    @pl.when(step == 1)
    def _():
        keys_in.wait()
        keys_out.start()
        values_in.wait()
        values_out.start()

    @pl.when(step == pl.num_programs(0) - 1)
    def _():
        keys_out.wait()
        values_out.wait()


def finish(place, gate_row, mixed, residual, key_main, key_late, value_main, value_late):
    tok_dev, features = residual.shape
    blocks = 4
    wide = features // blocks
    row_block = pl.BlockSpec((tok_dev, wide), lambda i: (0, i))
    item_block = pl.BlockSpec((mixed.shape[0] // blocks, 2, tok_dev, HD), lambda i: (i, 0, 0, 0))
    anywhere = pl.BlockSpec(memory_space=pl.ANY)
    whole = jax.ShapeDtypeStruct(residual.shape, jnp.bfloat16)
    return pl.pallas_call(
        finish_kernel,
        grid=(blocks,),
        in_specs=[
            pl.BlockSpec(memory_space=SMEM),
            pl.BlockSpec((1, wide), lambda i: (0, i)),
            item_block,
            row_block,
            anywhere,
            anywhere,
            anywhere,
            anywhere,
        ],
        out_specs=[row_block, anywhere, anywhere],
        out_shape=[whole, whole, whole],
        scratch_shapes=[
            pltpu.VMEM(residual.shape, jnp.bfloat16),
            pltpu.VMEM(residual.shape, jnp.bfloat16),
            pltpu.SemaphoreType.DMA((4,)),
        ],
        compiler_params=pltpu.CompilerParams(vmem_limit_bytes=VMEM_LIMIT),
        name="finish",
    )(place, gate_row, mixed, residual, key_main, key_late, value_main, value_late)


def moved(shard, *pairs):
    return lax.ppermute(shard, "queue", list(pairs))


def inner_pairs():
    return [(i, i + 1) for i in range(lax.axis_size("queue") - 1) if i + 1 != WRAP_TO]


def far_parts(own):
    share = own.shape[0] // len(RELAYS)
    parts = []
    for index, relay in enumerate(RELAYS):
        part = own[index * share : (index + 1) * share]
        if relay is None:
            parts.append(moved(part, (WRAP_TO - 1, WRAP_TO)))
        else:
            parts.append(moved(moved(part, (WRAP_TO - 1, relay)), (relay, WRAP_TO)))
    return parts


def exchange(items):
    return lax.all_to_all(items, "head", split_axis=0, concat_axis=0, tiled=True)


def shards(
    queries,
    key_proj,
    value_proj,
    residual,
    query_gain,
    key_gain,
    gate_table,
    noise_level,
    frame_reach,
):
    queue_pos, head_pos = lax.axis_index("queue"), lax.axis_index("head")
    place = jnp.stack([queue_pos, head_pos]).astype(jnp.int32)
    frame = queue_pos * FRAMES_GRP + head_pos // FRAME_SLOTS
    level = lax.dynamic_index_in_dim(noise_level, frame, 0, keepdims=False)
    gate_row = lax.dynamic_slice_in_dim(gate_table, level, 1, 0)
    items, key_norm = prep_keys(key_proj, value_proj, key_gain)
    value_main = moved(value_proj, *inner_pairs(), (WRAP_TO - 1, 0))
    key_main = moved(key_norm, *inner_pairs())
    own = exchange(items)
    query_items = prep_queries(queries, query_gain)
    own, query_items, value_main, key_main, gate_row, place = lax.optimization_barrier(
        (own, query_items, value_main, key_main, gate_row, place)
    )
    main = moved(own, *inner_pairs())
    far = far_parts(own)
    query_items = exchange(query_items)
    query_items, main, far, key_norm, value_main = lax.optimization_barrier(
        (query_items, main, far, key_norm, value_main)
    )
    key_late = moved(key_norm, (WRAP_TO - 1, WRAP_TO))
    value_late = moved(value_main, (0, WRAP_TO))
    mixed = attend(place, frame_reach, query_items, own, main, far)
    mixed, key_late, value_late = lax.optimization_barrier((mixed, key_late, value_late))
    mixed = exchange(mixed)
    advanced, key_cache, value_cache = finish(
        place, gate_row, mixed, residual, key_main, key_late, value_main, value_late
    )
    return (advanced, key_cache, value_cache)


def solution(mesh):
    return jax.shard_map(
        shards,
        mesh=mesh,
        in_specs=(
            P(("queue", "head"), None),
            P(("queue", "head"), None),
            P(("queue", "head"), None),
            P(("queue", "head"), None),
            P(),
            P(),
            P(),
            P(),
            P(),
        ),
        out_specs=(
            P(("queue", "head"), None),
            P(("queue", "head"), None),
            P(("queue", "head"), None),
        ),
        check_vma=False,
    )
```

time: 195 us -> 198 us (1.015)
  the two profiles are of different devices: /device:TPU:7 before, /device:TPU:32 now
where the time goes in v2:
time: 198 us; the launch traced here: 197 us
  Pallas kernels  65.9 us (33%)
  waiting for transfers between devices  62.8 us (32%)
  starting transfers between devices  33.8 us (17%)
  blocking collectives  30.2 us (15%)
  between operations  2.78 us (1%)
    pallas_call x1, Pallas kernels, attend(): pl.pallas_call(attend_kernel, grid=(heads, FRAMES_GRP), in_specs=[pl.Bloc...  52.8 us
    all_to_all x2, waiting for transfers between devices, exchange(): lax.all_to_all(items, 'head', split_axis=0, concat_axis=0, tiled=True)  38.3 us
    all_to_all x1, blocking collectives, exchange(): lax.all_to_all(items, 'head', split_axis=0, concat_axis=0, tiled=True)  30.2 us
    ppermute x12, waiting for transfers between devices, moved(): return lax.ppermute(shard, 'queue', list(pairs))  24.5 us
    ppermute x12, starting transfers between devices, moved(): return lax.ppermute(shard, 'queue', list(pairs))  18.8 us
    all_to_all x2, starting transfers between devices, exchange(): lax.all_to_all(items, 'head', split_axis=0, concat_axis=0, tiled=True)  15 us
    pallas_call x1, Pallas kernels, finish(): pl.pallas_call(finish_kernel, grid=(blocks,), in_specs=[pl.BlockSpec(memo...  5.03 us
    pallas_call x1, Pallas kernels, prep_keys(): pl.pallas_call(prep_keys_kernel, grid=(tok_dev // PREP_ROWS,), in_specs=[...  4.35 us
  transfers between devices with their start and end apart: 14, of which 3 were waited for; matrix products, arithmetic and copies ran while one was open for 1% of the time, Pallas kernels for 29%

profile of v2, /device:TPU:32, one launch (start us, length us, event | category | flops | bytes accessed | tf_op | source)
XLA Modules:
  0.0 197.4 jit_solution(5945935206229864171)
XLA Ops:
  0.6 0.0 copy-start
  0.6 4.3 %prep_keys.1 = (bf16[16,4,128,128]{3,2,1,0:T(8,128)(2,1)}, bf16[128,4096]{1,0:T(8,128)(2,1)}) custom-call(bf16[128,4096]{1,0:T(8,128)(2,1)} %k_ref.1, bf16[128,4096]{1,0:T(8,128)(2,1)} %v_ref.1, f32[1,4096]{1,0:T(1,128)} %bitcast.5), custom_call_target="tpu_custom_call" | custom-call | flops 4000000 | bytes 5000000 | tf_op jit(solution)/shard_map/prep_keys/pallas_call | solution.py:42
  5.0 10.4 %all-to-all-start = ((bf16[16,4,128,128]{3,2,1,0:T(8,128)(2,1)}), bf16[16,4,128,128]{3,2,1,0:T(8,128)(2,1)S(1)}, u32[]{:S(2)}, u32[]{:S(2)}) async-start(bf16[16,4,128,128]{3,2,1,0:T(8,128)(2,1)} %get-tuple-element.22), calls=%async_computation | async-start | bytes 4194304 | tf_op jit(solution)/shard_map/all_to_all | solution.py:338
  15.4 2.5 %collective-permute-start = (bf16[128,4096]{1,0:T(8,128)(2,1)}, bf16[128,4096]{1,0:T(8,128)(2,1)}, u32[]{:S(2)}, u32[]{:S(2)}) collective-permute-start(bf16[128,4096]{1,0:T(8,128)(2,1)} %v_ref.1), channel_id=1, source_target_pairs={{0,16},{16,32},{32,48},{48,64},{64,80},{80,96},{96,112},{128,144},... | collective-permute-start | bytes 3145736 | tf_op jit(solution)/shard_map/ppermute | solution.py:318
  17.9 4.0 %collective-permute-start.1 = (bf16[128,4096]{1,0:T(8,128)(2,1)}, bf16[128,4096]{1,0:T(8,128)(2,1)}, u32[]{:S(2)}, u32[]{:S(2)}) collective-permute-start(bf16[128,4096]{1,0:T(8,128)(2,1)} %get-tuple-element.35), channel_id=1, source_target_pairs={{0,16},{16,32},{32,48},{48,64},{64,80},{80,96},{96,112},{128,144},... | collective-permute-start | bytes 3145736 | tf_op jit(solution)/shard_map/ppermute | solution.py:318
  21.9 0.6 dynamic_slice.7
  24.4 3.7 %prep_queries.1 = bf16[16,2,128,128]{3,2,1,0:T(8,128)(2,1)} custom-call(bf16[128,4096]{1,0:T(8,128)(2,1)} %q_ref.1, f32[1,4096]{1,0:T(1,128)} %bitcast.6), custom_call_target="tpu_custom_call" | custom-call | flops 4000000 | bytes 3000000 | tf_op jit(solution)/shard_map/prep_queries/pallas_call | solution.py:66
  28.1 0.6 pad_add_fusion.place_ref
  28.7 0.6 constant_dynamic-slice_fusion.gate_ref
  29.3 0.0 collective-permute-done.value_main
  29.3 0.0 collective-permute-done.1.key_main
  29.3 38.3 %all-to-all-done.own_value.own_key = bf16[16,4,128,128]{3,2,1,0:T(8,128)(2,1)S(1)} async-done(((bf16[16,4,128,128]{3,2,1,0:T(8,128)(2,1)}), bf16[16,4,128,128]{3,2,1,0:T(8,128)(2,1)S(1)}, u32[]{:S(2)}, u32[]{:S(2)}) %all-to-all-start) | async-done | bytes 2097184 | tf_op jit(solution)/shard_map/all_to_all | solution.py:338
  67.6 2.6 %collective-permute-start.2 = (bf16[16,4,128,128]{3,2,1,0:T(8,128)(2,1)S(1)}, bf16[16,4,128,128]{3,2,1,0:T(8,128)(2,1)}, u32[]{:S(2)}, u32[]{:S(2)}) collective-permute-start(bf16[16,4,128,128]{3,2,1,0:T(8,128)(2,1)S(1)} %all-to-all-done.own_value.own_key), channel_id=1, source_target_pairs={{0,16},{16,32},{32,48},{48,64},{64,80},{80,96},{96,112},{128,144},... | collective-permute-start | bytes 6291464 | tf_op jit(solution)/shard_map/ppermute | solution.py:318
  70.2 4.5 %all-to-all-start.1 = ((bf16[16,2,128,128]{3,2,1,0:T(8,128)(2,1)}), bf16[16,2,128,128]{3,2,1,0:T(8,128)(2,1)}, u32[]{:S(2)}, u32[]{:S(2)}) async-start(bf16[16,2,128,128]{3,2,1,0:T(8,128)(2,1)} %prep_queries.1), calls=%async_computation.1 | async-start | bytes 2097152 | tf_op jit(solution)/shard_map/all_to_all | solution.py:338
  74.7 0.1 fusion
  74.9 0.7 collective-permute-start.8
  75.6 0.7 collective-permute-start.6
  76.3 0.7 collective-permute-start.4
  77.0 1.3 collective-permute-start.3
  78.3 1.3 collective-permute-start.9
  79.6 0.0 collective-permute-done.6
  79.6 1.3 collective-permute-start.7
  80.9 0.0 collective-permute-done.4
  80.9 1.3 collective-permute-start.5
  82.2 22.1 %collective-permute-done.3.refs_0_ = bf16[4,4,128,128]{3,2,1,0:T(8,128)(2,1)S(1)} collective-permute-done((bf16[4,4,128,128]{3,2,1,0:T(8,128)(2,1)S(1)}, bf16[4,4,128,128]{3,2,1,0:T(8,128)(2,1)S(1)}, u32[]{:S(2)}, u32[]{:S(2)}) %collective-permute-start.3) | collective-permute-done | bytes 524320 | tf_op jit(solution)/shard_map/ppermute | solution.py:318
  104.3 2.4 %collective-permute-done.9.refs_3_ = bf16[4,4,128,128]{3,2,1,0:T(8,128)(2,1)} collective-permute-done((bf16[4,4,128,128]{3,2,1,0:T(8,128)(2,1)S(1)}, bf16[4,4,128,128]{3,2,1,0:T(8,128)(2,1)}, u32[]{:S(2)}, u32[]{:S(2)}) %collective-permute-start.9) | collective-permute-done | bytes 524320 | tf_op jit(solution)/shard_map/ppermute | solution.py:318
  106.7 0.0 collective-permute-done.7.refs_2_
  106.7 1.3 collective-permute-start.10
  108.0 1.3 collective-permute-start.11
  109.3 52.8 %attend.1 = bf16[16,2,128,128]{3,2,1,0:T(8,128)(2,1)} custom-call(s32[2]{0:T(128)} %pad_add_fusion.place_ref, s32[64]{0:T(128)} %reach_ref.1, bf16[16,2,128,128]{3,2,1,0:T(8,128)(2,1)} %all-to-all-done.1.query_ref, bf16[16,4,128,128]{3,2,1,0:T(8,128)(2,1)} %copy-done.1, bf16[16,4,128,128]{3,2,1,0:T(8,128)(2,1)} %copy-done.1, ...), custom_call_target="tpu_custom_call" | custom-call | flops 16000000000 | bytes 6000000 | tf_op jit(solution)/shard_map/attend/pallas_call | solution.py:202
  162.2 30.2 %all_to_all.15.mixed_ref = bf16[16,2,128,128]{3,2,1,0:T(8,128)(2,1)} all-to-all(bf16[16,2,128,128]{3,2,1,0:T(8,128)(2,1)} %attend.1), channel_id=1, replica_groups=mesh['queue'=16,'head'=16] {'head'}, dimensions={0} | all-to-all | bytes 2097152 | tf_op jit(solution)/shard_map/all_to_all | solution.py:338
  192.4 5.0 %finish.1 = (bf16[128,4096]{1,0:T(8,128)(2,1)}, bf16[128,4096]{1,0:T(8,128)(2,1)}, bf16[128,4096]{1,0:T(8,128)(2,1)}) custom-call(s32[2]{0:T(128)} %pad_add_fusion.place_ref, f32[1,4096]{1,0:T(1,128)} %constant_dynamic-slice_fusion.gate_ref, bf16[16,2,128,128]{3,2,1,0:T(8,128)(2,1)} %all_to_all.15.mixed_ref, bf16[128,4096]{1,0:T(8,128)(2,1)} %residual_ref.1, ...), custom_call_target="tpu_custom_call" | custom-call | tf_op jit(solution)/shard_map/finish/pallas_call | solution.py:292
  (17 shorter events, 0.0 us)
Async XLA Ops:
  0.6 28.1 %copy-start = (f32[50,4096]{1,0:T(8,128)S(1)}, f32[50,4096]{1,0:T(8,128)}, u32[]{:S(2)}) copy-start(f32[50,4096]{1,0:T(8,128)} %param.15) | copy-start | bytes 2457604
  5.0 16.9 %copy-start.5 = (s32[64]{0:T(128)S(1)}, s32[64]{0:T(128)}, u32[]{:S(2)}) copy-start(s32[64]{0:T(128)} %param.16) | copy-start | bytes 772
  5.0 62.6 %all-to-all-start = ((bf16[16,4,128,128]{3,2,1,0:T(8,128)(2,1)}), bf16[16,4,128,128]{3,2,1,0:T(8,128)(2,1)S(1)}, u32[]{:S(2)}, u32[]{:S(2)}) async-start(bf16[16,4,128,128]{3,2,1,0:T(8,128)(2,1)} %get-tuple-element.22), calls=%async_computation | async-start | bytes 4194304 | tf_op jit(solution)/shard_map/all_to_all | solution.py:338
  15.4 13.9 %collective-permute-start = (bf16[128,4096]{1,0:T(8,128)(2,1)}, bf16[128,4096]{1,0:T(8,128)(2,1)}, u32[]{:S(2)}, u32[]{:S(2)}) collective-permute-start(bf16[128,4096]{1,0:T(8,128)(2,1)} %v_ref.1), channel_id=1, source_target_pairs={{0,16},{16,32},{32,48},{48,64},{64,80},{80,96},{96,112},{128,144},... | collective-permute-start | bytes 3145736 | tf_op jit(solution)/shard_map/ppermute | solution.py:318
  17.9 11.4 %collective-permute-start.1 = (bf16[128,4096]{1,0:T(8,128)(2,1)}, bf16[128,4096]{1,0:T(8,128)(2,1)}, u32[]{:S(2)}, u32[]{:S(2)}) collective-permute-start(bf16[128,4096]{1,0:T(8,128)(2,1)} %get-tuple-element.35), channel_id=1, source_target_pairs={{0,16},{16,32},{32,48},{48,64},{64,80},{80,96},{96,112},{128,144},... | collective-permute-start | bytes 3145736 | tf_op jit(solution)/shard_map/ppermute | solution.py:318
  67.6 7.3 %copy-start.1 = (bf16[16,4,128,128]{3,2,1,0:T(8,128)(2,1)}, bf16[16,4,128,128]{3,2,1,0:T(8,128)(2,1)S(1)}, u32[]{:S(2)}) copy-start(bf16[16,4,128,128]{3,2,1,0:T(8,128)(2,1)S(1)} %all-to-all-done.own_value.own_key) | copy-start | bytes 6291460
  67.6 39.1 %collective-permute-start.2 = (bf16[16,4,128,128]{3,2,1,0:T(8,128)(2,1)S(1)}, bf16[16,4,128,128]{3,2,1,0:T(8,128)(2,1)}, u32[]{:S(2)}, u32[]{:S(2)}) collective-permute-start(bf16[16,4,128,128]{3,2,1,0:T(8,128)(2,1)S(1)} %all-to-all-done.own_value.own_key), channel_id=1, source_target_pairs={{0,16},{16,32},{32,48},{48,64},{64,80},{80,96},{96,112},{128,144},... | collective-permute-start | bytes 6291464 | tf_op jit(solution)/shard_map/ppermute | solution.py:318
  70.2 36.6 %all-to-all-start.1 = ((bf16[16,2,128,128]{3,2,1,0:T(8,128)(2,1)}), bf16[16,2,128,128]{3,2,1,0:T(8,128)(2,1)}, u32[]{:S(2)}, u32[]{:S(2)}) async-start(bf16[16,2,128,128]{3,2,1,0:T(8,128)(2,1)} %prep_queries.1), calls=%async_computation.1 | async-start | bytes 2097152 | tf_op jit(solution)/shard_map/all_to_all | solution.py:338
  74.9 3.4 %collective-permute-start.8 = (bf16[4,4,128,128]{3,2,1,0:T(8,128)(2,1)S(1)}, bf16[4,4,128,128]{3,2,1,0:T(8,128)(2,1)S(1)}, u32[]{:S(2)}, u32[]{:S(2)}) collective-permute-start(bf16[4,4,128,128]{3,2,1,0:T(8,128)(2,1)S(1)} %get-tuple-element.41), channel_id=1, source_target_pairs={{112,80},{113,81},{114,82},{115,83},{116,84},{117,85},{118,86},{11... | collective-permute-start | bytes 1572872 | tf_op jit(solution)/shard_map/ppermute | solution.py:318
  75.6 4.0 %collective-permute-start.6 = (bf16[4,4,128,128]{3,2,1,0:T(8,128)(2,1)S(1)}, bf16[4,4,128,128]{3,2,1,0:T(8,128)(2,1)S(1)}, u32[]{:S(2)}, u32[]{:S(2)}) collective-permute-start(bf16[4,4,128,128]{3,2,1,0:T(8,128)(2,1)S(1)} %get-tuple-element.42), channel_id=1, source_target_pairs={{112,48},{113,49},{114,50},{115,51},{116,52},{117,53},{118,54},{11... | collective-permute-start | bytes 1572872 | tf_op jit(solution)/shard_map/ppermute | solution.py:318
  76.3 4.6 %collective-permute-start.4 = (bf16[4,4,128,128]{3,2,1,0:T(8,128)(2,1)S(1)}, bf16[4,4,128,128]{3,2,1,0:T(8,128)(2,1)S(1)}, u32[]{:S(2)}, u32[]{:S(2)}) collective-permute-start(bf16[4,4,128,128]{3,2,1,0:T(8,128)(2,1)S(1)} %get-tuple-element.43), channel_id=1, source_target_pairs={{112,0},{113,1},{114,2},{115,3},{116,4},{117,5},{118,6},{119,7},{1... | collective-permute-start | bytes 1572872 | tf_op jit(solution)/shard_map/ppermute | solution.py:318
  77.0 27.4 %collective-permute-start.3 = (bf16[4,4,128,128]{3,2,1,0:T(8,128)(2,1)S(1)}, bf16[4,4,128,128]{3,2,1,0:T(8,128)(2,1)S(1)}, u32[]{:S(2)}, u32[]{:S(2)}) collective-permute-start(bf16[4,4,128,128]{3,2,1,0:T(8,128)(2,1)S(1)} %get-tuple-element.44), channel_id=1, source_target_pairs={{112,128},{113,129},{114,130},{115,131},{116,132},{117,133},{118,1... | collective-permute-start | bytes 1572872 | tf_op jit(solution)/shard_map/ppermute | solution.py:318
  78.3 28.4 %collective-permute-start.9 = (bf16[4,4,128,128]{3,2,1,0:T(8,128)(2,1)S(1)}, bf16[4,4,128,128]{3,2,1,0:T(8,128)(2,1)}, u32[]{:S(2)}, u32[]{:S(2)}) collective-permute-start(bf16[4,4,128,128]{3,2,1,0:T(8,128)(2,1)S(1)} %collective-permute-done.8), channel_id=1, source_target_pairs={{80,128},{81,129},{82,130},{83,131},{84,132},{85,133},{86,134},{87... | collective-permute-start | bytes 1572872 | tf_op jit(solution)/shard_map/ppermute | solution.py:318
  79.6 27.1 %collective-permute-start.7 = (bf16[4,4,128,128]{3,2,1,0:T(8,128)(2,1)S(1)}, bf16[4,4,128,128]{3,2,1,0:T(8,128)(2,1)}, u32[]{:S(2)}, u32[]{:S(2)}) collective-permute-start(bf16[4,4,128,128]{3,2,1,0:T(8,128)(2,1)S(1)} %collective-permute-done.6), channel_id=1, source_target_pairs={{48,128},{49,129},{50,130},{51,131},{52,132},{53,133},{54,134},{55... | collective-permute-start | bytes 1572872 | tf_op jit(solution)/shard_map/ppermute | solution.py:318
  80.9 25.8 %collective-permute-start.5 = (bf16[4,4,128,128]{3,2,1,0:T(8,128)(2,1)S(1)}, bf16[4,4,128,128]{3,2,1,0:T(8,128)(2,1)}, u32[]{:S(2)}, u32[]{:S(2)}) collective-permute-start(bf16[4,4,128,128]{3,2,1,0:T(8,128)(2,1)S(1)} %collective-permute-done.4), channel_id=1, source_target_pairs={{0,128},{1,129},{2,130},{3,131},{4,132},{5,133},{6,134},{7,135},{8... | collective-permute-start | bytes 1572872 | tf_op jit(solution)/shard_map/ppermute | solution.py:318
  104.3 5.0 %copy-start.4 = (bf16[4,4,128,128]{3,2,1,0:T(8,128)(2,1)}, bf16[4,4,128,128]{3,2,1,0:T(8,128)(2,1)S(1)}, u32[]{:S(2)}) copy-start(bf16[4,4,128,128]{3,2,1,0:T(8,128)(2,1)S(1)} %collective-permute-done.3.refs_0_) | copy-start | bytes 1572868
  106.7 55.4 %collective-permute-start.10 = (bf16[128,4096]{1,0:T(8,128)(2,1)}, bf16[128,4096]{1,0:T(8,128)(2,1)S(1)}, u32[]{:S(2)}, u32[]{:S(2)}) collective-permute-start(bf16[128,4096]{1,0:T(8,128)(2,1)} %get-tuple-element.35), channel_id=1, source_target_pairs={{112,128},{113,129},{114,130},{115,131},{116,132},{117,133},{118,1... | collective-permute-start | bytes 3145736 | tf_op jit(solution)/shard_map/ppermute | solution.py:318
  108.0 54.1 %collective-permute-start.11 = (bf16[128,4096]{1,0:T(8,128)(2,1)}, bf16[128,4096]{1,0:T(8,128)(2,1)S(1)}, u32[]{:S(2)}, u32[]{:S(2)}) collective-permute-start(bf16[128,4096]{1,0:T(8,128)(2,1)} %collective-permute-done.value_main), channel_id=1, source_target_pairs={{0,128},{1,129},{2,130},{3,131},{4,132},{5,133},{6,134},{7,135},{8... | collective-permute-start | bytes 3145736 | tf_op jit(solution)/shard_map/ppermute | solution.py:318
  162.1 30.2 %copy-start.2 = (bf16[128,4096]{1,0:T(8,128)(2,1)}, bf16[128,4096]{1,0:T(8,128)(2,1)S(1)}, u32[]{:S(2)}) copy-start(bf16[128,4096]{1,0:T(8,128)(2,1)S(1)} %collective-permute-done.10.key_late) | copy-start | bytes 3145732
  162.2 30.2 %copy-start.3 = (bf16[128,4096]{1,0:T(8,128)(2,1)}, bf16[128,4096]{1,0:T(8,128)(2,1)S(1)}, u32[]{:S(2)}) copy-start(bf16[128,4096]{1,0:T(8,128)(2,1)S(1)} %collective-permute-done.11.value_late) | copy-start | bytes 3145732

commit v3 on v1

v3 whole, which is shorter than its diff:
```python
import math

import jax
import jax.numpy as jnp
from jax import lax
from jax.experimental import pallas as pl
from jax.experimental.pallas import tpu as pltpu
from jax.sharding import PartitionSpec as P

HD = 128
FRAMES_GRP = 4
FRAME_SLOTS = 4
PREP_ROWS = 64
CACHE_PARTS = 4
QUERY_ROWS = 256
WRAP_TO = 8
KEY_RELAY, VALUE_RELAY = 3, 0
LOG2E = 1.4426950408889634
SMEM = pltpu.SMEM
VMEM_LIMIT = 60 * 1024 * 1024


def normalize(token_rows, gain_row):
    values = token_rows.astype(jnp.float32)
    square = jnp.mean(values * values, axis=-1, keepdims=True)
    return (values * lax.rsqrt(square + 1e-06) * gain_row).astype(jnp.bfloat16)


def prep_kernel(q_ref, k_ref, v_ref, qg_ref, kg_ref, early_ref, late_ref, key_ref):
    value = v_ref[...]
    key_norm = normalize(k_ref[...], kg_ref[...])
    query_norm = normalize(q_ref[...], qg_ref[...])
    key_ref[...] = key_norm
    for head in range(q_ref.shape[1] // HD):
        at = slice(head * HD, (head + 1) * HD)
        slot, second = head // 2, head % 2
        early_ref[slot, 2 * second] = value[:, at]
        early_ref[slot, 2 * second + 1] = key_norm[:, at]
        if second:
            late_ref[slot, 0] = query_norm[:, at]
        else:
            early_ref[slot, 4] = query_norm[:, at]


def prepare(queries, key_proj, value_proj, query_gain, key_gain):
    tok_dev, features = queries.shape
    slots = features // HD // 2
    row_block = pl.BlockSpec((PREP_ROWS, features), lambda i: (i, 0))
    gain_block = pl.BlockSpec((1, features), lambda i: (0, 0))
    return pl.pallas_call(
        prep_kernel,
        grid=(tok_dev // PREP_ROWS,),
        in_specs=[row_block, row_block, row_block, gain_block, gain_block],
        out_specs=[
            pl.BlockSpec((slots, 5, PREP_ROWS, HD), lambda i: (0, 0, i, 0)),
            pl.BlockSpec((slots, 1, PREP_ROWS, HD), lambda i: (0, 0, i, 0)),
            row_block,
        ],
        out_shape=[
            jax.ShapeDtypeStruct((slots, 5, tok_dev, HD), jnp.bfloat16),
            jax.ShapeDtypeStruct((slots, 1, tok_dev, HD), jnp.bfloat16),
            jax.ShapeDtypeStruct((tok_dev, features), jnp.bfloat16),
        ],
        compiler_params=pltpu.CompilerParams(vmem_limit_bytes=VMEM_LIMIT),
        cost_estimate=pl.CostEstimate(flops=8_000_000, bytes_accessed=8_000_000, transcendentals=0),
        name="prep",
    )(queries, key_proj, value_proj, query_gain.reshape(1, -1), key_gain.reshape(1, -1))


def attend_kernel(
    place_ref,
    reach_ref,
    query_ref,
    own_value,
    own_key,
    *refs,
):
    *priors, out_ref, total_ref, held_ref, sems = refs
    frame = pl.program_id(0)
    queue_pos = place_ref[0]
    main, *far = priors

    @pl.when((frame == 0) & ((queue_pos != WRAP_TO) | (not far)))
    def _():
        load = pltpu.make_async_copy(main, held_ref, sems.at[0])
        load.start()
        load.wait()

    if far:

        @pl.when((frame == 0) & (queue_pos == WRAP_TO))
        def _():
            loads = [
                pltpu.make_async_copy(part, held_ref.at[:, at], sems.at[at])
                for at, part in enumerate(far)
            ]
            for load in loads:
                load.start()
            for load in loads:
                load.wait()

    prior_value, prior_key = held_ref.at[:, 0], held_ref.at[:, 1]
    lowest = jnp.where(queue_pos > 0, -FRAMES_GRP, 0)
    lower = jnp.maximum(frame - reach_ref[queue_pos * FRAMES_GRP + frame], lowest)
    own_from = jnp.maximum(lower, 0)
    prior_from = jnp.minimum(lower, 0) + FRAMES_GRP
    rows = query_ref.shape[0] * query_ref.shape[1]
    scale = LOG2E / math.sqrt(HD)

    def scores_of(query, key):
        return lax.dot_general(
            query, key, (((1,), (1,)), ((), ())), preferred_element_type=jnp.float32
        )

    def block(ref, start, count):
        slots = ref[pl.ds(start * FRAME_SLOTS, count * FRAME_SLOTS)]
        return slots.reshape(count * rows, HD)

    def plain(parts):
        pairs = [
            (block(key_ref, start, FRAMES_GRP - start), block(value_ref, start, FRAMES_GRP - start))
            for key_ref, value_ref, start in parts
        ]
        query = query_ref[...].reshape(rows, HD)
        for low in range(0, rows, QUERY_ROWS):
            at = slice(low, low + QUERY_ROWS)
            lanes, mixed = None, None
            for key, value in pairs:
                weights = jnp.exp2(scores_of(query[at], key) * scale)
                part = jnp.dot(
                    weights.astype(jnp.bfloat16), value, preferred_element_type=jnp.float32
                )
                mixed = part if mixed is None else mixed + part
                for col in range(0, weights.shape[1], HD):
                    one = weights[:, col : col + HD]
                    lanes = one if lanes is None else lanes + one
            total = jnp.sum(lanes, axis=1, keepdims=True)
            slot = low // out_ref.shape[1]
            count = QUERY_ROWS // out_ref.shape[1]
            result = (mixed / total).astype(jnp.bfloat16)
            out_ref[slot : slot + count] = result.reshape(count, *out_ref.shape[1:])
            total_ref[at] = total

    for start in range(FRAMES_GRP):

        @pl.when((own_from == start) & (prior_from == FRAMES_GRP))
        def _(start=start):
            plain([(own_key, own_value, start)])

        @pl.when(prior_from == start)
        def _(start=start):
            plain([(own_key, own_value, 0), (prior_key, prior_value, start)])

    def store(mixed, total):
        out_ref[...] = (mixed / total).astype(jnp.bfloat16).reshape(out_ref.shape)

    total = total_ref[...]
    inside = (jnp.max(total) < 1e37) & (jnp.min(total) > 1e-25)

    @pl.when(jnp.logical_not(inside))
    def _():
        query = query_ref[...].reshape(rows, HD)

        def tile(key, value, carry):
            highest, total, mixed = carry
            scores = scores_of(query, key)
            raised = jnp.maximum(highest, jnp.max(scores, axis=1, keepdims=True))
            fade = jnp.exp2((highest - raised) * scale)
            weights = jnp.exp2((scores - raised) * scale)
            total = total * fade + jnp.sum(weights, axis=1, keepdims=True)
            part = jnp.dot(weights.astype(jnp.bfloat16), value, preferred_element_type=jnp.float32)
            return raised, total, mixed * fade + part

        def own_tile(step, carry):
            return tile(block(own_key, step, 1), block(own_value, step, 1), carry)

        def prior_tile(step, carry):
            return tile(block(prior_key, step, 1), block(prior_value, step, 1), carry)

        start = jnp.full((rows, 1), -1e30, jnp.float32)
        carry = (start, jnp.zeros_like(start), jnp.zeros((rows, HD), jnp.float32))
        carry = lax.fori_loop(own_from, FRAMES_GRP, own_tile, carry)
        _, total, mixed = lax.fori_loop(prior_from, FRAMES_GRP, prior_tile, carry)
        store(mixed, total)


def attend(place, frame_reach, query, own, *priors):
    query, query_at = query
    own, own_at = own
    slots, _, tok_dev, _ = own.shape
    rows = FRAME_SLOTS * tok_dev

    def whole(index):
        return pl.BlockSpec((slots, None, tok_dev, HD), lambda i: (0, index, 0, 0))

    return pl.pallas_call(
        attend_kernel,
        grid=(FRAMES_GRP,),
        in_specs=[
            pl.BlockSpec(memory_space=SMEM),
            pl.BlockSpec(memory_space=SMEM),
            pl.BlockSpec((FRAME_SLOTS, None, tok_dev, HD), lambda i: (i, query_at, 0, 0)),
            whole(own_at),
            whole(own_at + 1),
            *[pl.BlockSpec(memory_space=pl.ANY) for _ in priors],
        ],
        out_specs=pl.BlockSpec((FRAME_SLOTS, tok_dev, HD), lambda i: (i, 0, 0)),
        out_shape=jax.ShapeDtypeStruct((slots, tok_dev, HD), jnp.bfloat16),
        scratch_shapes=[
            pltpu.VMEM((rows, 1), jnp.float32),
            pltpu.VMEM(priors[0].shape, jnp.bfloat16),
            pltpu.SemaphoreType.DMA((2,)),
        ],
        compiler_params=pltpu.CompilerParams(vmem_limit_bytes=VMEM_LIMIT),
        cost_estimate=pl.CostEstimate(
            flops=8_000_000_000, bytes_accessed=3_000_000, transcendentals=8_000_000
        ),
        name="attend",
    )(place, frame_reach, query, own, own, *priors)


def place_kernel(
    place_ref,
    key_main,
    key_late,
    value_main,
    value_late,
    key_out,
    value_out,
    key_held,
    value_held,
    sems,
):
    late = place_ref[0] == WRAP_TO
    rows = key_held.shape[0] // CACHE_PARTS
    for part in range(CACHE_PARTS):
        at = pl.ds(part * rows, rows)

        def load(source, held, index, at=at, part=part):
            return pltpu.make_async_copy(source.at[at], held.at[at], sems.at[index, part])

        @pl.when(late)
        def _(load=load):
            load(key_late, key_held, 0).start()
            load(value_late, value_held, 1).start()

        @pl.when(jnp.logical_not(late))
        def _(load=load):
            load(key_main, key_held, 0).start()
            load(value_main, value_held, 1).start()

    stores = []
    for part in range(CACHE_PARTS):
        at = pl.ds(part * rows, rows)
        for index, source, held, out in (
            (0, key_main, key_held, key_out),
            (1, value_main, value_held, value_out),
        ):
            pltpu.make_async_copy(source.at[at], held.at[at], sems.at[index, part]).wait()
            store = pltpu.make_async_copy(held.at[at], out.at[at], sems.at[index + 2, part])
            store.start()
            stores.append(store)
    for store in stores:
        store.wait()


def place_caches(place, key_main, key_late, value_main, value_late):
    anywhere = pl.BlockSpec(memory_space=pl.ANY)
    whole = jax.ShapeDtypeStruct(key_main.shape, jnp.bfloat16)
    return pl.pallas_call(
        place_kernel,
        in_specs=[pl.BlockSpec(memory_space=SMEM), anywhere, anywhere, anywhere, anywhere],
        out_specs=[anywhere, anywhere],
        out_shape=[whole, whole],
        scratch_shapes=[
            pltpu.VMEM(key_main.shape, jnp.bfloat16),
            pltpu.VMEM(key_main.shape, jnp.bfloat16),
            pltpu.SemaphoreType.DMA((4, CACHE_PARTS)),
        ],
        compiler_params=pltpu.CompilerParams(vmem_limit_bytes=VMEM_LIMIT),
        cost_estimate=pl.CostEstimate(flops=0, bytes_accessed=4_000_000, transcendentals=0),
        name="place_caches",
    )(place, key_main, key_late, value_main, value_late)


def finish_kernel(gate_ref, first_ref, second_ref, residual_ref, out_ref):
    for head in range(residual_ref.shape[1] // HD):
        source = second_ref if head % 2 else first_ref
        at = slice(head * HD, (head + 1) * HD)
        mixed = gate_ref[:, at] * source[head // 2].astype(jnp.float32)
        out_ref[:, at] = (residual_ref[:, at].astype(jnp.float32) + mixed).astype(jnp.bfloat16)


def finish(gate_row, first, second, residual):
    tok_dev, features = residual.shape
    blocks = 2
    wide = features // blocks
    row_block = pl.BlockSpec((tok_dev, wide), lambda i: (0, i))
    item_block = pl.BlockSpec((first.shape[0] // blocks, tok_dev, HD), lambda i: (i, 0, 0))
    return pl.pallas_call(
        finish_kernel,
        grid=(blocks,),
        in_specs=[
            pl.BlockSpec((1, wide), lambda i: (0, i)),
            item_block,
            item_block,
            row_block,
        ],
        out_specs=row_block,
        out_shape=jax.ShapeDtypeStruct(residual.shape, jnp.bfloat16),
        compiler_params=pltpu.CompilerParams(vmem_limit_bytes=VMEM_LIMIT),
        name="finish",
    )(gate_row, first, second, residual)


def moved(shard, *pairs):
    return lax.ppermute(shard, "queue", list(pairs))


def inner_pairs():
    return [(i, i + 1) for i in range(lax.axis_size("queue") - 1) if i + 1 != WRAP_TO]


def exchange(items):
    return lax.all_to_all(items, "head", split_axis=0, concat_axis=0, tiled=True)


def shards(
    queries,
    key_proj,
    value_proj,
    residual,
    query_gain,
    key_gain,
    gate_table,
    noise_level,
    frame_reach,
):
    queue_pos, head_pos = lax.axis_index("queue"), lax.axis_index("head")
    place = jnp.stack([queue_pos, head_pos]).astype(jnp.int32)
    frame = queue_pos * FRAMES_GRP + head_pos // FRAME_SLOTS
    level = lax.dynamic_index_in_dim(noise_level, frame, 0, keepdims=False)
    gate_row = lax.dynamic_slice_in_dim(gate_table, level, 1, 0)
    early, late, key_norm = prepare(queries, key_proj, value_proj, query_gain, key_gain)
    inner = inner_pairs()
    every = (*inner, (WRAP_TO - 1, WRAP_TO))
    value_main = moved(value_proj, *inner)
    key_main = moved(key_norm, *inner)
    value_half = moved(value_proj, (WRAP_TO - 1, VALUE_RELAY))
    key_half = moved(key_norm, (WRAP_TO - 1, KEY_RELAY))
    early = exchange(early)
    early, late, value_main, key_main, value_half, key_half, gate_row, place = (
        lax.optimization_barrier(
            (early, late, value_main, key_main, value_half, key_half, gate_row, place)
        )
    )
    key_late = moved(key_half, (KEY_RELAY, WRAP_TO))
    value_late = moved(value_half, (VALUE_RELAY, WRAP_TO))
    wrap = (WRAP_TO - 1, WRAP_TO)
    prior_first = moved(early[:, 0:2], *every)
    prior_second = moved(early[:, 2:4], *inner)
    far_second = [moved(early[:, 2], wrap), moved(early[:, 3], wrap)]
    late = exchange(late)
    first = attend(place, frame_reach, (early, 4), (early, 0), prior_first)
    first, late, prior_second, key_late, value_late = lax.optimization_barrier(
        (first, late, prior_second, key_late, value_late)
    )
    first = exchange(first)
    second = attend(place, frame_reach, (late, 0), (early, 2), prior_second, *far_second)
    first, second = lax.optimization_barrier((first, second))
    second = exchange(second)
    key_cache, value_cache = place_caches(place, key_main, key_late, value_main, value_late)
    second, key_cache, value_cache = lax.optimization_barrier((second, key_cache, value_cache))
    advanced = finish(gate_row, first, second, residual)
    return (advanced, key_cache, value_cache)


def solution(mesh):
    return jax.shard_map(
        shards,
        mesh=mesh,
        in_specs=(
            P(("queue", "head"), None),
            P(("queue", "head"), None),
            P(("queue", "head"), None),
            P(("queue", "head"), None),
            P(),
            P(),
            P(),
            P(),
            P(),
        ),
        out_specs=(
            P(("queue", "head"), None),
            P(("queue", "head"), None),
            P(("queue", "head"), None),
        ),
        check_vma=False,
    )
```

time: 195 us -> 196 us (level); the launches traced: 194 us -> 198 us
  blocking collectives: 49.2 us -> 0 us
  Pallas kernels: 42.6 us -> 67.8 us
  starting transfers between devices: 46 us -> 68.5 us
  waiting for transfers between devices: 43 us -> 52.4 us
  local copies, waits for them, and re-layouts: 12.6 us -> 6.48 us
  between operations: 0.77 us -> 2.75 us
    all_to_all x1 -> x0, blocking collectives: 49.2 us -> none  [exchange(): lax.all_to_all(items, 'head', split_axis=0, concat_axis=0, tiled=True)]
    pallas_call x2, Pallas kernels: 37.4 us -> 57.9 us  [attend(): pl.pallas_call(attend_kernel, grid=(FRAMES_GRP,), in_specs=[pl.BlockSpec(...]
    ppermute x4 -> x10, starting transfers between devices: 22.3 us -> 38.5 us  [moved(): return lax.ppermute(shard, 'queue', list(pairs))]
    ppermute x4 -> x10, waiting for transfers between devices: 0.33 us -> 9.57 us  [moved(): return lax.ppermute(shard, 'queue', list(pairs))]
    unnamed x26 -> x14, local copies, waits for them, and re-layouts: 10.5 us -> 2.4 us
    all_to_all x3 -> x4, starting transfers between devices: 23.7 us -> 30.1 us  [exchange(): lax.all_to_all(items, 'head', split_axis=0, concat_axis=0, tiled=True)]
    pallas_call x1 -> x2, Pallas kernels: 2.42 us -> 5.58 us  [the longest x1 3.06 us: place_caches(): pl.pallas_call(place_kernel, in_specs=[pl.BlockSpec(memory_space=SMEM), a...]
    all_to_all x3 -> x4, waiting for transfers between devices: 42.6 us -> 42.8 us  [exchange(): lax.all_to_all(items, 'head', split_axis=0, concat_axis=0, tiled=True)]
  transfers between devices with their start and end apart: 7 -> 14, of which waited for: 3 -> 5; matrix products, arithmetic and copies ran while one was open for 1% -> 1% of each run, Pallas kernels for 19% -> 31%
where the time goes in v3:
time: 196 us; the launch traced here: 198 us
  starting transfers between devices  68.5 us (35%)
  Pallas kernels  67.8 us (35%)
  waiting for transfers between devices  52.4 us (27%)
  local copies, waits for them, and re-layouts  6.48 us (3%)
  between operations  2.75 us (1%)
    pallas_call x2, Pallas kernels, attend(): pl.pallas_call(attend_kernel, grid=(FRAMES_GRP,), in_specs=[pl.BlockSpec(...  57.9 us
    all_to_all x4, waiting for transfers between devices, exchange(): lax.all_to_all(items, 'head', split_axis=0, concat_axis=0, tiled=True)  42.8 us
    ppermute x10, starting transfers between devices, moved(): return lax.ppermute(shard, 'queue', list(pairs))  38.5 us
    all_to_all x4, starting transfers between devices, exchange(): lax.all_to_all(items, 'head', split_axis=0, concat_axis=0, tiled=True)  30.1 us
    ppermute x10, waiting for transfers between devices, moved(): return lax.ppermute(shard, 'queue', list(pairs))  9.57 us
    pallas_call x1, Pallas kernels, prepare(): pl.pallas_call(prep_kernel, grid=(tok_dev // PREP_ROWS,), in_specs=[row_b...  4.31 us
  transfers between devices with their start and end apart: 14, of which 5 were waited for; matrix products, arithmetic and copies ran while one was open for 1% of the time, Pallas kernels for 31%

profile of v3, /device:TPU:7, one launch (start us, length us, event | category | flops | bytes accessed | tf_op | source)
XLA Modules:
  0.0 198.5 jit_solution(5007618045085424606)
XLA Ops:
  0.6 4.3 %prep.1 = (bf16[16,5,128,128]{3,2,1,0:T(8,128)(2,1)}, bf16[16,1,128,128]{3,2,1,0:T(8,128)(2,1)}, bf16[128,4096]{1,0:T(8,128)(2,1)}) custom-call(bf16[128,4096]{1,0:T(8,128)(2,1)} %q_ref.1, bf16[128,4096]{1,0:T(8,128)(2,1)} %k_ref.1, bf16[128,4096]{1,0:T(8,128)(2,1)} %v_ref.1, f32[1,4096]{1,0:T(1,128)} %bitcast.9, f32[1,4096]{1,0:T(1,128)} %bitcast.10), custom_call_target="tpu_custom_call" | custom-call | flops 8000000 | bytes 8000000 | tf_op jit(solution)/shard_map/prep/pallas_call | solution.py:50
  5.0 11.1 %all-to-all-start = ((bf16[16,5,128,128]{3,2,1,0:T(8,128)(2,1)}), bf16[16,5,128,128]{3,2,1,0:T(8,128)(2,1)S(1)}, u32[]{:S(2)}, u32[]{:S(2)}) async-start(bf16[16,5,128,128]{3,2,1,0:T(8,128)(2,1)} %get-tuple-element.26), calls=%async_computation | async-start | bytes 5242880 | tf_op jit(solution)/shard_map/all_to_all | solution.py:325
  16.0 1.3 collective-permute-start
  17.3 1.3 collective-permute-start.1
  18.6 7.8 %collective-permute-start.2 = (bf16[128,4096]{1,0:T(8,128)(2,1)}, bf16[128,4096]{1,0:T(8,128)(2,1)}, u32[]{:S(2)}, u32[]{:S(2)}) collective-permute-start(bf16[128,4096]{1,0:T(8,128)(2,1)} %v_ref.1), channel_id=1, source_target_pairs={{112,0},{113,1},{114,2},{115,3},{116,4},{117,5},{118,6},{119,7},{1... | collective-permute-start | bytes 3145736 | tf_op jit(solution)/shard_map/ppermute | solution.py:317
  26.4 2.3 %collective-permute-start.3 = (bf16[128,4096]{1,0:T(8,128)(2,1)}, bf16[128,4096]{1,0:T(8,128)(2,1)}, u32[]{:S(2)}, u32[]{:S(2)}) collective-permute-start(bf16[128,4096]{1,0:T(8,128)(2,1)} %get-tuple-element.28), channel_id=1, source_target_pairs={{112,48},{113,49},{114,50},{115,51},{116,52},{117,53},{118,54},{11... | collective-permute-start | bytes 3145736 | tf_op jit(solution)/shard_map/ppermute | solution.py:317
  28.7 0.6 dynamic_slice.7
  31.3 0.6 pad_add_fusion.place_ref
  31.8 0.6 constant_dynamic-slice_fusion.gate_ref
  32.5 5.0 %collective-permute-done.2 = bf16[128,4096]{1,0:T(8,128)(2,1)} collective-permute-done((bf16[128,4096]{1,0:T(8,128)(2,1)}, bf16[128,4096]{1,0:T(8,128)(2,1)}, u32[]{:S(2)}, u32[]{:S(2)}) %collective-permute-start.2) | collective-permute-done | bytes 1048608 | tf_op jit(solution)/shard_map/ppermute | solution.py:317
  37.4 2.3 %collective-permute-done.3 = bf16[128,4096]{1,0:T(8,128)(2,1)} collective-permute-done((bf16[128,4096]{1,0:T(8,128)(2,1)}, bf16[128,4096]{1,0:T(8,128)(2,1)}, u32[]{:S(2)}, u32[]{:S(2)}) %collective-permute-start.3) | collective-permute-done | bytes 1048608 | tf_op jit(solution)/shard_map/ppermute | solution.py:317
  39.7 33.5 %all-to-all-done.query_ref.own_value.own_key = bf16[16,5,128,128]{3,2,1,0:T(8,128)(2,1)S(1)} async-done(((bf16[16,5,128,128]{3,2,1,0:T(8,128)(2,1)}), bf16[16,5,128,128]{3,2,1,0:T(8,128)(2,1)S(1)}, u32[]{:S(2)}, u32[]{:S(2)}) %all-to-all-start) | async-done | bytes 2621472 | tf_op jit(solution)/shard_map/all_to_all | solution.py:325
  73.2 1.7 fusion
  74.9 9.8 %collective-permute-start.4 = (bf16[16,2,128,128]{3,2,1,0:T(8,128)(2,1)}, bf16[16,2,128,128]{3,2,1,0:T(8,128)(2,1)}, u32[]{:S(2)}, u32[]{:S(2)}) collective-permute-start(bf16[16,2,128,128]{3,2,1,0:T(8,128)(2,1)} %get-tuple-element.52), channel_id=1, source_target_pairs={{0,16},{16,32},{32,48},{48,64},{64,80},{80,96},{96,112},{128,144},... | collective-permute-start | bytes 3145736 | tf_op jit(solution)/shard_map/ppermute | solution.py:317
  84.7 1.3 collective-permute-start.5
  86.0 1.7 collective-permute-start.6
  87.7 1.6 collective-permute-start.7
  89.3 4.2 %all-to-all-start.1 = ((bf16[16,1,128,128]{3,2,1,0:T(8,128)(2,1)}), bf16[16,1,128,128]{3,2,1,0:T(8,128)(2,1)}, u32[]{:S(2)}, u32[]{:S(2)}) async-start(bf16[16,1,128,128]{3,2,1,0:T(8,128)(2,1)} %get-tuple-element.32), calls=%async_computation.1 | async-start | bytes 1048576 | tf_op jit(solution)/shard_map/all_to_all | solution.py:325
  93.6 1.1 slice_bitcast_fusion
  94.7 4.6 %collective-permute-start.8 = (bf16[16,128,128]{2,1,0:T(8,128)(2,1)}, bf16[16,128,128]{2,1,0:T(8,128)(2,1)S(1)}, u32[]{:S(2)}, u32[]{:S(2)}) collective-permute-start(bf16[16,128,128]{2,1,0:T(8,128)(2,1)} %get-tuple-element.50), channel_id=1, source_target_pairs={{112,128},{113,129},{114,130},{115,131},{116,132},{117,133},{118,1... | collective-permute-start | bytes 1572872 | tf_op jit(solution)/shard_map/ppermute | solution.py:317
  99.3 2.3 %collective-permute-done.4.refs_0_ = bf16[16,2,128,128]{3,2,1,0:T(8,128)(2,1)} collective-permute-done((bf16[16,2,128,128]{3,2,1,0:T(8,128)(2,1)}, bf16[16,2,128,128]{3,2,1,0:T(8,128)(2,1)}, u32[]{:S(2)}, u32[]{:S(2)}) %collective-permute-start.4) | collective-permute-done | bytes 1048608 | tf_op jit(solution)/shard_map/ppermute | solution.py:317
  101.6 6.8 %collective-permute-start.9 = (bf16[16,128,128]{2,1,0:T(8,128)(2,1)}, bf16[16,128,128]{2,1,0:T(8,128)(2,1)S(1)}, u32[]{:S(2)}, u32[]{:S(2)}) collective-permute-start(bf16[16,128,128]{2,1,0:T(8,128)(2,1)} %get-tuple-element.49), channel_id=1, source_target_pairs={{112,128},{113,129},{114,130},{115,131},{116,132},{117,133},{118,1... | collective-permute-start | bytes 1572872 | tf_op jit(solution)/shard_map/ppermute | solution.py:317
  108.4 29.0 %attend.2 = bf16[16,128,128]{2,1,0:T(8,128)(2,1)} custom-call(s32[2]{0:T(128)} %pad_add_fusion.place_ref, s32[64]{0:T(128)} %reach_ref.3, bf16[16,5,128,128]{3,2,1,0:T(8,128)(2,1)} %copy-done.1, bf16[16,5,128,128]{3,2,1,0:T(8,128)(2,1)} %copy-done.1, bf16[16,5,128,128]{3,2,1,0:T(8,128)(2,1)} %copy-done.1, ...), custom_call_target="tpu_custom_call" | custom-call | flops 8000000000 | bytes 3000000 | tf_op jit(solution)/shard_map/attend/pallas_call | solution.py:196
  137.5 5.7 %all-to-all-start.2 = ((bf16[16,128,128]{2,1,0:T(8,128)(2,1)}), bf16[16,128,128]{2,1,0:T(8,128)(2,1)S(1)}, u32[]{:S(2)}, u32[]{:S(2)}) async-start(bf16[16,128,128]{2,1,0:T(8,128)(2,1)} %attend.2), calls=%async_computation.2 | async-start | bytes 1048576 | tf_op jit(solution)/shard_map/all_to_all | solution.py:325
  143.2 0.8 copy-done.4
  144.0 0.8 copy-done.5
  144.8 28.8 %attend.3 = bf16[16,128,128]{2,1,0:T(8,128)(2,1)} custom-call(s32[2]{0:T(128)} %pad_add_fusion.place_ref, s32[64]{0:T(128)} %reach_ref.3, bf16[16,1,128,128]{3,2,1,0:T(8,128)(2,1)} %all-to-all-done.1.query_ref, bf16[16,5,128,128]{3,2,1,0:T(8,128)(2,1)} %copy-done.1, bf16[16,5,128,128]{3,2,1,0:T(8,128)(2,1)} %copy-done.1, ...), custom_call_target="tpu_custom_call" | custom-call | flops 8000000000 | bytes 3000000 | tf_op jit(solution)/shard_map/attend/pallas_call | solution.py:196
  173.7 9.1 %all-to-all-start.3 = ((bf16[16,128,128]{2,1,0:T(8,128)(2,1)}), bf16[16,128,128]{2,1,0:T(8,128)(2,1)S(1)}, u32[]{:S(2)}, u32[]{:S(2)}) async-start(bf16[16,128,128]{2,1,0:T(8,128)(2,1)} %attend.3), calls=%async_computation.3 | async-start | bytes 1048576 | tf_op jit(solution)/shard_map/all_to_all | solution.py:325
  182.7 3.1 %place_caches.1 = (bf16[128,4096]{1,0:T(8,128)(2,1)}, bf16[128,4096]{1,0:T(8,128)(2,1)}) custom-call(s32[2]{0:T(128)} %pad_add_fusion.place_ref, bf16[128,4096]{1,0:T(8,128)(2,1)} %collective-permute-done.1.key_main, bf16[128,4096]{1,0:T(8,128)(2,1)} %collective-permute-done.6.key_late, bf16[128,4096]{1,0:T(8,128)(2,1)} %collective-permute-done.value_main, ...), custom_call_target="tpu_custom_call" | custom-call | bytes 4000000 | tf_op jit(solution)/shard_map/place_caches/pallas_call | solution.py:270
  185.8 9.3 %all-to-all-done.3.second_ref = bf16[16,128,128]{2,1,0:T(8,128)(2,1)S(1)} async-done(((bf16[16,128,128]{2,1,0:T(8,128)(2,1)}), bf16[16,128,128]{2,1,0:T(8,128)(2,1)S(1)}, u32[]{:S(2)}, u32[]{:S(2)}) %all-to-all-start.3) | async-done | bytes 524320 | tf_op jit(solution)/shard_map/all_to_all | solution.py:325
  195.2 0.8 copy-done.3
  196.0 2.5 %finish.1 = bf16[128,4096]{1,0:T(8,128)(2,1)} custom-call(f32[1,4096]{1,0:T(1,128)} %constant_dynamic-slice_fusion.gate_ref, bf16[16,128,128]{2,1,0:T(8,128)(2,1)} %copy-done.2, bf16[16,128,128]{2,1,0:T(8,128)(2,1)} %copy-done.3, bf16[128,4096]{1,0:T(8,128)(2,1)} %residual_ref.1), custom_call_target="tpu_custom_call" | custom-call | tf_op jit(solution)/shard_map/finish/pallas_call | solution.py:300
  (20 shorter events, 0.1 us)
Async XLA Ops:
  0.6 31.2 %copy-start = (f32[50,4096]{1,0:T(8,128)S(1)}, f32[50,4096]{1,0:T(8,128)}, u32[]{:S(2)}) copy-start(f32[50,4096]{1,0:T(8,128)} %param.15) | copy-start | bytes 2457604
  5.0 23.8 %copy-start.6 = (s32[64]{0:T(128)S(1)}, s32[64]{0:T(128)}, u32[]{:S(2)}) copy-start(s32[64]{0:T(128)} %param.16) | copy-start | bytes 772
  5.0 68.2 %all-to-all-start = ((bf16[16,5,128,128]{3,2,1,0:T(8,128)(2,1)}), bf16[16,5,128,128]{3,2,1,0:T(8,128)(2,1)S(1)}, u32[]{:S(2)}, u32[]{:S(2)}) async-start(bf16[16,5,128,128]{3,2,1,0:T(8,128)(2,1)} %get-tuple-element.26), calls=%async_computation | async-start | bytes 5242880 | tf_op jit(solution)/shard_map/all_to_all | solution.py:325
  16.0 16.4 %collective-permute-start = (bf16[128,4096]{1,0:T(8,128)(2,1)}, bf16[128,4096]{1,0:T(8,128)(2,1)}, u32[]{:S(2)}, u32[]{:S(2)}) collective-permute-start(bf16[128,4096]{1,0:T(8,128)(2,1)} %v_ref.1), channel_id=1, source_target_pairs={{0,16},{16,32},{32,48},{48,64},{64,80},{80,96},{96,112},{128,144},... | collective-permute-start | bytes 3145736 | tf_op jit(solution)/shard_map/ppermute | solution.py:317
  17.3 15.1 %collective-permute-start.1 = (bf16[128,4096]{1,0:T(8,128)(2,1)}, bf16[128,4096]{1,0:T(8,128)(2,1)}, u32[]{:S(2)}, u32[]{:S(2)}) collective-permute-start(bf16[128,4096]{1,0:T(8,128)(2,1)} %get-tuple-element.28), channel_id=1, source_target_pairs={{0,16},{16,32},{32,48},{48,64},{64,80},{80,96},{96,112},{128,144},... | collective-permute-start | bytes 3145736 | tf_op jit(solution)/shard_map/ppermute | solution.py:317
  18.6 18.8 %collective-permute-start.2 = (bf16[128,4096]{1,0:T(8,128)(2,1)}, bf16[128,4096]{1,0:T(8,128)(2,1)}, u32[]{:S(2)}, u32[]{:S(2)}) collective-permute-start(bf16[128,4096]{1,0:T(8,128)(2,1)} %v_ref.1), channel_id=1, source_target_pairs={{112,0},{113,1},{114,2},{115,3},{116,4},{117,5},{118,6},{119,7},{1... | collective-permute-start | bytes 3145736 | tf_op jit(solution)/shard_map/ppermute | solution.py:317
  26.4 13.3 %collective-permute-start.3 = (bf16[128,4096]{1,0:T(8,128)(2,1)}, bf16[128,4096]{1,0:T(8,128)(2,1)}, u32[]{:S(2)}, u32[]{:S(2)}) collective-permute-start(bf16[128,4096]{1,0:T(8,128)(2,1)} %get-tuple-element.28), channel_id=1, source_target_pairs={{112,48},{113,49},{114,50},{115,51},{116,52},{117,53},{118,54},{11... | collective-permute-start | bytes 3145736 | tf_op jit(solution)/shard_map/ppermute | solution.py:317
  73.2 20.4 %copy-start.1 = (bf16[16,5,128,128]{3,2,1,0:T(8,128)(2,1)}, bf16[16,5,128,128]{3,2,1,0:T(8,128)(2,1)S(1)}, u32[]{:S(2)}) copy-start(bf16[16,5,128,128]{3,2,1,0:T(8,128)(2,1)S(1)} %all-to-all-done.query_ref.own_value.own_key) | copy-start | bytes 7864324
  74.9 26.7 %collective-permute-start.4 = (bf16[16,2,128,128]{3,2,1,0:T(8,128)(2,1)}, bf16[16,2,128,128]{3,2,1,0:T(8,128)(2,1)}, u32[]{:S(2)}, u32[]{:S(2)}) collective-permute-start(bf16[16,2,128,128]{3,2,1,0:T(8,128)(2,1)} %get-tuple-element.52), channel_id=1, source_target_pairs={{0,16},{16,32},{32,48},{48,64},{64,80},{80,96},{96,112},{128,144},... | collective-permute-start | bytes 3145736 | tf_op jit(solution)/shard_map/ppermute | solution.py:317
  84.7 52.7 %collective-permute-start.5 = (bf16[16,2,128,128]{3,2,1,0:T(8,128)(2,1)}, bf16[16,2,128,128]{3,2,1,0:T(8,128)(2,1)}, u32[]{:S(2)}, u32[]{:S(2)}) collective-permute-start(bf16[16,2,128,128]{3,2,1,0:T(8,128)(2,1)} %get-tuple-element.51), channel_id=1, source_target_pairs={{0,16},{16,32},{32,48},{48,64},{64,80},{80,96},{96,112},{128,144},... | collective-permute-start | bytes 3145736 | tf_op jit(solution)/shard_map/ppermute | solution.py:317
  86.0 51.5 %collective-permute-start.6 = (bf16[128,4096]{1,0:T(8,128)(2,1)}, bf16[128,4096]{1,0:T(8,128)(2,1)}, u32[]{:S(2)}, u32[]{:S(2)}) collective-permute-start(bf16[128,4096]{1,0:T(8,128)(2,1)} %collective-permute-done.3), channel_id=1, source_target_pairs={{48,128},{49,129},{50,130},{51,131},{52,132},{53,133},{54,134},{55... | collective-permute-start | bytes 3145736 | tf_op jit(solution)/shard_map/ppermute | solution.py:317
  87.7 49.8 %collective-permute-start.7 = (bf16[128,4096]{1,0:T(8,128)(2,1)}, bf16[128,4096]{1,0:T(8,128)(2,1)}, u32[]{:S(2)}, u32[]{:S(2)}) collective-permute-start(bf16[128,4096]{1,0:T(8,128)(2,1)} %collective-permute-done.2), channel_id=1, source_target_pairs={{0,128},{1,129},{2,130},{3,131},{4,132},{5,133},{6,134},{7,135},{8... | collective-permute-start | bytes 3145736 | tf_op jit(solution)/shard_map/ppermute | solution.py:317
  89.3 48.1 %all-to-all-start.1 = ((bf16[16,1,128,128]{3,2,1,0:T(8,128)(2,1)}), bf16[16,1,128,128]{3,2,1,0:T(8,128)(2,1)}, u32[]{:S(2)}, u32[]{:S(2)}) async-start(bf16[16,1,128,128]{3,2,1,0:T(8,128)(2,1)} %get-tuple-element.32), calls=%async_computation.1 | async-start | bytes 1048576 | tf_op jit(solution)/shard_map/all_to_all | solution.py:325
  94.7 48.5 %collective-permute-start.8 = (bf16[16,128,128]{2,1,0:T(8,128)(2,1)}, bf16[16,128,128]{2,1,0:T(8,128)(2,1)S(1)}, u32[]{:S(2)}, u32[]{:S(2)}) collective-permute-start(bf16[16,128,128]{2,1,0:T(8,128)(2,1)} %get-tuple-element.50), channel_id=1, source_target_pairs={{112,128},{113,129},{114,130},{115,131},{116,132},{117,133},{118,1... | collective-permute-start | bytes 1572872 | tf_op jit(solution)/shard_map/ppermute | solution.py:317
  101.6 41.6 %collective-permute-start.9 = (bf16[16,128,128]{2,1,0:T(8,128)(2,1)}, bf16[16,128,128]{2,1,0:T(8,128)(2,1)S(1)}, u32[]{:S(2)}, u32[]{:S(2)}) collective-permute-start(bf16[16,128,128]{2,1,0:T(8,128)(2,1)} %get-tuple-element.49), channel_id=1, source_target_pairs={{112,128},{113,129},{114,130},{115,131},{116,132},{117,133},{118,1... | collective-permute-start | bytes 1572872 | tf_op jit(solution)/shard_map/ppermute | solution.py:317
  137.5 36.2 %all-to-all-start.2 = ((bf16[16,128,128]{2,1,0:T(8,128)(2,1)}), bf16[16,128,128]{2,1,0:T(8,128)(2,1)S(1)}, u32[]{:S(2)}, u32[]{:S(2)}) async-start(bf16[16,128,128]{2,1,0:T(8,128)(2,1)} %attend.2), calls=%async_computation.2 | async-start | bytes 1048576 | tf_op jit(solution)/shard_map/all_to_all | solution.py:325
  143.2 0.8 copy-start.4
  144.0 0.8 copy-start.5
  173.7 12.2 %copy-start.2 = (bf16[16,128,128]{2,1,0:T(8,128)(2,1)}, bf16[16,128,128]{2,1,0:T(8,128)(2,1)S(1)}, u32[]{:S(2)}) copy-start(bf16[16,128,128]{2,1,0:T(8,128)(2,1)S(1)} %all-to-all-done.2.first_ref) | copy-start | bytes 1572868
  173.7 21.5 %all-to-all-start.3 = ((bf16[16,128,128]{2,1,0:T(8,128)(2,1)}), bf16[16,128,128]{2,1,0:T(8,128)(2,1)S(1)}, u32[]{:S(2)}, u32[]{:S(2)}) async-start(bf16[16,128,128]{2,1,0:T(8,128)(2,1)} %attend.3), calls=%async_computation.3 | async-start | bytes 1048576 | tf_op jit(solution)/shard_map/all_to_all | solution.py:325
  195.1 0.8 copy-start.3
